TPU v7x, 256 devices: a whole 4x4x8 slice. The times are simulated.
256 devices in a mesh: py: 8 (over z), px: 8 (over y, core), vert: 4 (over x).
Axes of the slice: x: 4, y: 4, z: 8, core: 2. Of those that a mesh axis runs over, the one named last changes fastest.
Arguments:
- warped_image: float32 [8, 3072, 3072], P('vert', 'py', 'px'), may hold values from -6 to 6
- variance: float32 [8, 3072, 3072], P('vert', 'py', 'px'), may hold values from 0.25 to 4
- kernel_factors: float32 [8, 2304, 246], P('vert', ('py', 'px')), may hold values from -1 to 1
- cell_source: int32 [8, 2304], P('vert', ('py', 'px')), may hold values from 0 to 2303, as said below
- coverage: int32 [8, 2304], P('vert', ('py', 'px')), may hold values 0 or 1
Outputs:
- coadd: float32 [3072, 3072], P(('py', 'vert'), 'px')
- weight_sum: float32 [3072, 3072], P(('py', 'vert'), 'px')
Inputs may be any that keep to these rules, and one draw needn't show every extreme that they name: `cell_source`: for each visit every storage index of a kernel cell is named exactly once; storage indices s * 36 to s * 36 + 35 belong to storage owner s, and for each visit and patch every storage owner holds either none or exactly 6 of that patch's cells.
All inputs are finite; a program needn't handle non-finite values. No bound on the sum of `coverage` on one device may be relied on, other than what follows from the above.
Results may differ from a plain program's by a relative error of at most 0.000098.
Values sent between devices are 32-bit elements; how exact they have to be, the bound alone decides.
A program may use at most 64 MiB of HBM per device.

v0:
```python
import jax
import jax.numpy as jnp
from jax import lax
from jax.sharding import PartitionSpec as P

TAPS = 41
RANK = 3
CELL = 64
HALF = 20


weight_floor = 0.5
highest = lax.Precision.HIGHEST


def with_halo(block, sides, width):
    for axis, dim in sides:
        count = lax.axis_size(axis)
        forward = [(i, i + 1) for i in range(count - 1)]
        backward = [(target, source) for source, target in forward]
        low = lax.ppermute(
            lax.slice_in_dim(block, block.shape[dim] - width, None, axis=dim), axis, forward
        )
        high = lax.ppermute(lax.slice_in_dim(block, 0, width, axis=dim), axis, backward)
        block = jnp.concatenate([low, block, high], axis=dim)
    return block


def band_table():
    shift_ids = jnp.arange(TAPS)[:, None, None]
    row_ids = jnp.arange(CELL)[None, :, None]
    col_ids = jnp.arange(CELL + 2 * HALF)[None, None, :]
    return (col_ids - row_ids == shift_ids).astype(jnp.float32)


def cell_windows(padded, rows_cells, cols_cells):
    height = rows_cells * CELL
    width = cols_cells * CELL
    span = 2 * HALF
    extended = jnp.pad(padded, ((0, CELL - span), (0, CELL - span)))
    upper = extended[:height].reshape(rows_cells, CELL, width + CELL)
    lower = extended[CELL : height + CELL].reshape(rows_cells, CELL, width + CELL)[:, :span]
    stripes = jnp.concatenate([upper, lower], axis=1)
    left = stripes[:, :, :width].reshape(rows_cells, CELL + span, cols_cells, CELL)
    right = stripes[:, :, CELL : width + CELL].reshape(rows_cells, CELL + span, cols_cells, CELL)[
        ..., :span
    ]
    tiles = jnp.concatenate([left, right], axis=3)
    return tiles.transpose(0, 2, 1, 3).reshape(rows_cells * cols_cells, CELL + span, CELL + span)


def convolve_cells(tiles, factors):
    shaped = factors.reshape(-1, RANK, 2, TAPS)
    table = band_table()
    row_bands = jnp.einsum("crs,sik->crik", shaped[:, :, 0], table, precision=highest)
    col_bands = jnp.einsum("crs,sjl->crjl", shaped[:, :, 1], table, precision=highest)
    partial_pass = jnp.einsum("crik,ckl->cril", row_bands, tiles, precision=highest)
    return jnp.einsum("cril,crjl->cij", partial_pass, col_bands, precision=highest)


def assemble(blocks, rows_cells, cols_cells):
    return (
        blocks.reshape(rows_cells, cols_cells, CELL, CELL)
        .transpose(0, 2, 1, 3)
        .reshape(rows_cells * CELL, cols_cells * CELL)
    )


def select_rows(portion, position, wanted):
    length = portion.shape[1]
    inside = wanted & (position >= 0) & (position < length)
    chosen = jnp.take_along_axis(portion, jnp.clip(position, 0, length - 1)[:, :, None], axis=1)
    return jnp.where(inside[:, :, None], chosen, 0.0)


def shards(warped_image, variance, kernel_factors, cell_source, coverage):
    visits = warped_image.shape[0]
    side = warped_image.shape[1]
    per_side = side // CELL
    padded = with_halo(warped_image, (("py", 1), ("px", 2)), HALF)
    factors = select_rows(
        lax.all_gather(kernel_factors, ("py", "px"), axis=1, tiled=True),
        cell_source,
        cell_source >= 0,
    )
    convolved_list = []
    for visit_index in range(visits):
        tiles = cell_windows(padded[visit_index], per_side, per_side)
        convolved_list.append(
            assemble(convolve_cells(tiles, factors[visit_index]), per_side, per_side)
        )
    convolved = jnp.stack(convolved_list)
    cover = coverage.reshape(visits, per_side, per_side).astype(jnp.float32)
    cover_pixels = jnp.repeat(jnp.repeat(cover, CELL, axis=1), CELL, axis=2)
    weights = cover_pixels / variance
    numerator_term = jnp.sum(weights * convolved, axis=0)
    denominator_term = jnp.sum(weights, axis=0)
    numerator_full, denominator_full = lax.psum((numerator_term, denominator_term), "vert")
    share = side // lax.axis_size("vert")
    first_row = lax.axis_index("vert") * share
    numerator = lax.dynamic_slice_in_dim(numerator_full, first_row, share, 0)
    denominator = lax.dynamic_slice_in_dim(denominator_full, first_row, share, 0)
    weight_sum = jnp.maximum(denominator, weight_floor)
    coadd = numerator / weight_sum
    return (coadd, weight_sum)


def solution(mesh):
    placed = (
        P("vert", "py", "px"),
        P("vert", "py", "px"),
        P("vert", ("py", "px"), None),
        P("vert", ("py", "px")),
        P("vert", ("py", "px")),
    )
    return jax.shard_map(
        shards,
        mesh=mesh,
        in_specs=placed,
        out_specs=(P(("py", "vert"), "px"), P(("py", "vert"), "px")),
        check_vma=False,
    )
```

profile of v0, /device:TPU:1, one launch (start us, length us, event | category | flops | bytes accessed | tf_op | source)
XLA Modules:
  0.0 195.4 jit_solution(2648064675240045673)
XLA Ops:
  8.9 4.4 %collective-permute-start = (f32[2,20,384]{2,1,0:T(8,128)S(1)}, f32[2,20,384]{2,1,0:T(8,128)S(1)}, u32[]{:S(2)}, u32[]{:S(2)}) collective-permute-start(f32[2,20,384]{2,1,0:T(8,128)S(1)} %get-tuple-element.16), channel_id=1, source_target_pairs={{0,32},{32,64},{64,96},{96,128},{128,160},{160,192},{192,224},{1,3... | collective-permute-start | bytes 184328 | tf_op jit(solution)/shard_map/ppermute | solution.py:21
  13.3 1.3 collective-permute-start.1
  16.1 2.7 %copy.47 = f32[2,384,384]{1,2,0:T(8,128)} copy(f32[2,384,384]{2,1,0:T(8,128)} %param.6) | data formatting | bytes 2359296 | tf_op args[1]
  19.3 4.4 %collective-permute-start.2 = (f32[2,424,20]{2,1,0:T(8,128)S(1)}, f32[2,424,20]{2,1,0:T(8,128)S(1)}, u32[]{:S(2)}, u32[]{:S(2)}) collective-permute-start(f32[2,424,20]{2,1,0:T(8,128)S(1)} %get-tuple-element.10), channel_id=1, source_target_pairs={{0,4},{4,8},{8,12},{12,16},{16,20},{20,24},{24,28},{1,5},{5,9},{9,... | collective-permute-start | bytes 203528 | tf_op jit(solution)/shard_map/ppermute | solution.py:21
  23.8 1.9 collective-permute-start.3
  25.7 3.6 %collective-permute-done.2 = f32[2,424,20]{2,1,0:T(8,128)S(1)} collective-permute-done((f32[2,424,20]{2,1,0:T(8,128)S(1)}, f32[2,424,20]{2,1,0:T(8,128)S(1)}, u32[]{:S(2)}, u32[]{:S(2)}) %collective-permute-start.2) | collective-permute-done | bytes 67872 | tf_op jit(solution)/shard_map/ppermute | solution.py:21
  29.3 4.9 %collective-permute-done.3 = f32[2,424,20]{2,1,0:T(8,128)S(1)} collective-permute-done((f32[2,424,20]{2,1,0:T(8,128)S(1)}, f32[2,424,20]{2,1,0:T(8,128)S(1)}, u32[]{:S(2)}, u32[]{:S(2)}) %collective-permute-start.3) | collective-permute-done | bytes 67872 | tf_op jit(solution)/shard_map/ppermute | solution.py:24
  35.1 1.2 pad_slice_fusion.5
  36.7 1.4 copy.51
  38.1 2.0 %slice.104 = f32[6,104,6,40]{1,3,2,0:T(8,128)} slice(f32[6,104,6,64]{1,3,2,0:T(8,128)} %bitcast.98), slice={[0:6], [0:104], [0:6], [0:40]} | slice | bytes 1198080 | tf_op jit(solution)/shard_map/slice | solution.py:45
  41.6 1.3 fusion.18
  42.8 1.4 copy.59
  44.2 2.2 %slice.112 = f32[6,104,6,40]{1,3,2,0:T(8,128)} slice(f32[6,104,6,64]{1,3,2,0:T(8,128)} %bitcast.99), slice={[0:6], [0:104], [0:6], [0:40]} | slice | bytes 1198080 | tf_op jit(solution)/shard_map/slice | solution.py:45
  46.4 1.6 copy.58
  48.0 1.4 pad_maximum_fusion
  49.5 44.8 %all-gather.2.cloned.1.call-done = f32[2,2304,246]{2,0,1:T(2,128)} async-done(((f32[2,36,246]{2,0,1:T(2,128)}), f32[2,2304,246]{2,0,1:T(2,128)}) %all-gather.2.cloned.1.call-update) | async-done | bytes 4534288 | tf_op jit(solution)/shard_map/all_gather | solution.py:82
  94.3 4.9 %copy.48 = f32[2,2304,246]{2,1,0:T(8,128)} copy(f32[2,2304,246]{2,0,1:T(2,128)} %all-gather.2.cloned.1.call-done) | data formatting | bytes 9068544 | tf_op jit(solution)/shard_map/all_gather | solution.py:82
  99.2 3.7 %gather_fusion = f32[72,246]{1,0:T(8,128)S(1)} fusion(f32[2,2304,246]{2,1,0:T(8,128)} %copy.48, s32[72]{0:T(128)S(1)} %reshape.86), kind=kCustom, calls=%fused_computation | custom fusion | bytes 142272 | tf_op jit(solution)/shard_map/jit(take_along_axis)/gather | solution.py:72
  103.9 1.7 fusion.15
  105.7 1.7 fusion.13
  107.4 4.4 %fusion.6 = f32[36,3,64,104]{3,2,1,0:T(8,128)S(1)} fusion(f32[36,104,104,1]{1,2,3,0:T(8,128)S(1)} %bitcast.89, f32[36,3,64,104]{3,0,2,1:T(8,128)S(1)} %fusion.15), kind=kOutput, calls=%fused_computation.7 | convolution fusion | flops 897122304 | bytes 7308288 | tf_op jit(solution)/shard_map/crik,ckl->cril/dot_general | solution.py:57
  111.8 4.8 %fusion.4 = f32[36,64,64,1]{2,1,3,0:T(8,128)S(1)} fusion(f32[36,3,64,104]{3,2,1,0:T(8,128)S(1)} %fusion.6, f32[36,3,64,104]{3,0,2,1:T(8,128)S(1)} %fusion.13), kind=kOutput, calls=%fused_computation.5 | convolution fusion | flops 552075264 | bytes 6340608 | tf_op jit(solution)/shard_map/cril,crjl->cij/dot_general | solution.py:58
  117.3 1.2 stack_reshape.6
  118.5 1.3 copy.65
  120.8 1.7 fusion.11
  122.6 1.7 fusion.9
  124.3 4.5 %fusion.2 = f32[36,3,64,104]{3,2,1,0:T(8,128)S(1)} fusion(f32[36,104,104,1]{1,2,3,0:T(8,128)S(1)} %bitcast.88, f32[36,3,64,104]{3,0,2,1:T(8,128)S(1)} %fusion.11), kind=kOutput, calls=%fused_computation.3 | convolution fusion | flops 897122304 | bytes 7308288 | tf_op jit(solution)/shard_map/crik,ckl->cril/dot_general | solution.py:57
  128.8 4.8 %fusion = f32[36,64,64,1]{2,1,3,0:T(8,128)S(1)} fusion(f32[36,3,64,104]{3,2,1,0:T(8,128)S(1)} %fusion.2, f32[36,3,64,104]{3,0,2,1:T(8,128)S(1)} %fusion.9), kind=kOutput, calls=%fused_computation.1 | convolution fusion | flops 552075264 | bytes 6340608 | tf_op jit(solution)/shard_map/cril,crjl->cij/dot_general | solution.py:58
  135.5 1.3 copy.66
  136.8 1.2 fusion.24
  138.1 47.7 %all-reduce.5.cloned.1.call-done = (f32[384,384]{0,1:T(8,128)}, f32[384,384]{0,1:T(8,128)}) async-done(((f32[384,384]{0,1:T(8,128)}, f32[384,384]{0,1:T(8,128)}), (f32[384,384]{0,1:T(8,128)}, f32[384,384]{0,1:T(8,128)})) %all-reduce.5.cloned.1.call-update) | async-done | bytes 1179664 | tf_op jit(solution)/shard_map/psum | solution.py:98
  185.7 1.3 dynamic-slice_maximum_fusion
  (49 shorter events, 12.6 us)
Async XLA Ops:
  7.2 12.0 %copy-start.1 = (f32[2,384,384]{2,1,0:T(8,128)S(1)}, f32[2,384,384]{2,1,0:T(8,128)}, u32[]{:S(2)}) copy-start(f32[2,384,384]{2,1,0:T(8,128)} %param.5) | copy-start | bytes 3538948
  7.2 11.6 %copy-start.5 = (s32[2,36]{1,0:T(2,128)S(1)}, s32[2,36]{1,0:T(2,128)}, u32[]{:S(2)}) copy-start(s32[2,36]{1,0:T(2,128)} %param.9) | copy-start | bytes 868
  7.2 87.1 %all-gather.2.cloned.1.call-start = ((), (), s32[]{:S(2)}) async-start(), calls=%async_computation | async-start | bytes 4792320 | tf_op jit(solution)/shard_map/all_gather | solution.py:82
  7.9 177.8 %all-reduce.5.cloned.1.call-start = ((), (), s32[]{:S(2)}) async-start(), calls=%async_computation.1 | async-start | bytes 2359296 | tf_op jit(solution)/shard_map/psum | solution.py:98
  8.9 10.2 %collective-permute-start = (f32[2,20,384]{2,1,0:T(8,128)S(1)}, f32[2,20,384]{2,1,0:T(8,128)S(1)}, u32[]{:S(2)}, u32[]{:S(2)}) collective-permute-start(f32[2,20,384]{2,1,0:T(8,128)S(1)} %get-tuple-element.16), channel_id=1, source_target_pairs={{0,32},{32,64},{64,96},{96,128},{128,160},{160,192},{192,224},{1,3... | collective-permute-start | bytes 184328 | tf_op jit(solution)/shard_map/ppermute | solution.py:21
  13.3 5.8 %collective-permute-start.1 = (f32[2,20,384]{2,1,0:T(8,128)S(1)}, f32[2,20,384]{2,1,0:T(8,128)S(1)}, u32[]{:S(2)}, u32[]{:S(2)}) collective-permute-start(f32[2,20,384]{2,1,0:T(8,128)S(1)} %get-tuple-element.17), channel_id=1, source_target_pairs={{32,0},{64,32},{96,64},{128,96},{160,128},{192,160},{224,192},{33,... | collective-permute-start | bytes 184328 | tf_op jit(solution)/shard_map/ppermute | solution.py:24
  19.3 10.0 %collective-permute-start.2 = (f32[2,424,20]{2,1,0:T(8,128)S(1)}, f32[2,424,20]{2,1,0:T(8,128)S(1)}, u32[]{:S(2)}, u32[]{:S(2)}) collective-permute-start(f32[2,424,20]{2,1,0:T(8,128)S(1)} %get-tuple-element.10), channel_id=1, source_target_pairs={{0,4},{4,8},{8,12},{12,16},{16,20},{20,24},{24,28},{1,5},{5,9},{9,... | collective-permute-start | bytes 203528 | tf_op jit(solution)/shard_map/ppermute | solution.py:21
  23.8 10.4 %collective-permute-start.3 = (f32[2,424,20]{2,1,0:T(8,128)S(1)}, f32[2,424,20]{2,1,0:T(8,128)S(1)}, u32[]{:S(2)}, u32[]{:S(2)}) collective-permute-start(f32[2,424,20]{2,1,0:T(8,128)S(1)} %get-tuple-element.11), channel_id=1, source_target_pairs={{4,0},{8,4},{12,8},{16,12},{20,16},{24,20},{28,24},{5,1},{9,5},{13... | collective-permute-start | bytes 203528 | tf_op jit(solution)/shard_map/ppermute | solution.py:24
  44.2 3.7 %copy-start.3 = (f32[6,104,6,40]{1,3,2,0:T(8,128)S(1)}, f32[6,104,6,40]{1,3,2,0:T(8,128)}, u32[]{:S(2)}) copy-start(f32[6,104,6,40]{1,3,2,0:T(8,128)} %slice.104) | copy-start | bytes 1797124
  48.0 1.4 copy-start.4
  105.6 1.7 copy-start
  134.3 2.5 %copy-start.2 = (f32[2,384,384]{1,2,0:T(8,128)S(1)}, f32[2,384,384]{1,2,0:T(8,128)}, u32[]{:S(2)}) copy-start(f32[2,384,384]{1,2,0:T(8,128)} %copy.47) | copy-start | bytes 3538948
Sparse Core Ops, SparseCore 0:
  10.8 83.5 all-gather.1
  138.2 47.5 all-reduce.4
where the time goes:
time: 196 us; the launch traced here: 195 us
  waiting for transfers between devices  102 us (52%)
  local copies, waits for them, and re-layouts  34 us (17%)
  matrix products  25.3 us (13%)
  between operations  14.4 us (7%)
  starting transfers between devices  12.1 us (6%)
  other arithmetic  7.98 us (4%)
    psum x1, waiting for transfers between devices, shards(): lax.psum((numerator_term, denominator_term), 'vert')  47.7 us
    all_gather x1, waiting for transfers between devices, shards(): lax.all_gather(kernel_factors, ('py', 'px'), axis=1, tiled=True)  44.8 us
    dot_general x2, matrix products, convolve_cells(): jnp.einsum('cril,crjl->cij', partial_pass, col_bands, precision=highest)  9.62 us
    dot_general x2, matrix products, convolve_cells(): jnp.einsum('crik,ckl->cril', row_bands, tiles, precision=highest)  8.91 us
    ppermute x2, starting transfers between devices, with_halo(): lax.ppermute(lax.slice_in_dim(block, block.shape[dim] - width, None, axis...  8.82 us
    slice x4, local copies, waits for them, and re-layouts, cell_windows(): stripes[:, :, CELL:width + CELL]  7.05 us
    another operation x4, local copies, waits for them, and re-layouts, shards(): convolved = jnp.stack(convolved_list)  4.99 us
    all_gather x1, local copies, waits for them, and re-layouts, shards(): lax.all_gather(kernel_factors, ('py', 'px'), axis=1, tiled=True)  4.9 us
  transfers between devices with their start and end apart: 6, of which 4 were waited for; matrix products, arithmetic and copies ran while one was open for 11% of the time, Pallas kernels for 0%

commit v1 on v0

v1 whole, which is shorter than its diff:
```python
import jax
import jax.numpy as jnp
from jax import lax
from jax.experimental import pallas as pl
from jax.experimental.pallas import tpu as pltpu
from jax.sharding import PartitionSpec as P

TAPS = 41
RANK = 3
CELL = 64
HALF = 20
CPS = 6
SIDE = 384
CELLS = 36
PAD = 40
FACT = 246
BORDER = 24
ROWS = SIDE + 2 * BORDER
WINDOW = 80
SHARE = 96
CHUNK = 72
N_VERT = 4
N_LINE = 8

MESH = pl.DeviceIdType.MESH
f32 = jnp.float32
bf16 = jnp.bfloat16


def lanes(rows):
    return lax.broadcasted_iota(jnp.int32, (rows, 128), 1)


def turn(x, shift):
    shift = shift % 128
    return x if shift == 0 else pltpu.roll(x, shift, 1)


def split(x):
    high = x.astype(bf16)
    low = (x - high.astype(f32)).astype(bf16)
    return high, low


def kernel(
    img, var, fac, cs, cov,
    coadd, wsum,
    ext, zbuf, csb, sbuf, rbuf, taps, xs, xr, thi, tlo, weight, num, den, rnum, rden,
    local_sem, zsend, zrecv, csend, crecv, ssend, srecv, hsend, hrecv, xsend, xrecv,
    nsend, nrecv, dsend, drecv,
):
    a = lax.axis_index("py")
    b = lax.axis_index("px")
    x = lax.axis_index("vert")

    def at_py(d):
        return {"py": lax.rem(a + d, N_LINE)}

    def at_px(d):
        return {"px": lax.rem(b + d, N_LINE)}

    def remote(src, dst, send, recv, device):
        return pltpu.make_async_remote_copy(
            src_ref=src, dst_ref=dst, send_sem=send, recv_sem=recv,
            device_id=device, device_id_type=MESH,
        )

    barrier = pltpu.get_barrier_semaphore()
    for d in (1, N_LINE - 1):
        pl.semaphore_signal(barrier, inc=1, device_id=at_py(d), device_id_type=MESH)
    for d in range(1, N_LINE):
        pl.semaphore_signal(barrier, inc=1, device_id=at_px(d), device_id_type=MESH)
    for d in range(1, N_VERT):
        pl.semaphore_signal(
            barrier, inc=1, device_id={"vert": lax.rem(x + d, N_VERT)}, device_id_type=MESH
        )

    own_image = pltpu.make_async_copy(img, ext.at[:, pl.ds(BORDER, SIDE), :], local_sem)
    own_image.start()

    for v in range(2):
        zbuf[v, 0] = jnp.zeros((PAD, 256), f32)
        zbuf[v, 0, 0:CELLS, 0:FACT] = fac[v]
        first = zbuf[v, 0, :, 0:128]
        second = zbuf[v, 0, :, 128:256]
        zbuf[v, 0, :, 128:256] = jnp.where(lanes(PAD) < 5, turn(first, 5), turn(second, 5))
    csb[0] = jnp.full((8, 128), -1.0, f32)
    csb[0, 0:2, 0:CELLS] = cs[...].astype(f32)

    pl.semaphore_wait(barrier, 2 + N_LINE - 1 + N_VERT - 1)

    cs_copies = [
        remote(csb.at[0], csb.at[N_LINE - d], csend.at[d], crecv.at[N_LINE - d], at_px(d))
        for d in range(1, N_LINE)
    ]

    def ring(v, source, target, d):
        return remote(
            zbuf.at[v, source], zbuf.at[v, target], zsend.at[v, target], zrecv.at[v, target],
            at_py(d),
        )

    up_chain = ((0, 1), (1, 2), (2, 3), (3, 4))
    down_chain = ((0, 7), (7, 6), (6, 5))
    z_up = [[ring(v, s, t, 1) for s, t in up_chain] for v in range(2)]
    z_down = [[ring(v, s, t, N_LINE - 1) for s, t in down_chain] for v in range(2)]
    h_down = remote(
        img.at[:, pl.ds(SIDE - BORDER, BORDER), :], ext.at[:, pl.ds(0, BORDER), :],
        hsend.at[0], hrecv.at[0], at_py(1),
    )
    h_up = remote(
        img.at[:, pl.ds(0, BORDER), :], ext.at[:, pl.ds(BORDER + SIDE, BORDER), :],
        hsend.at[1], hrecv.at[1], at_py(N_LINE - 1),
    )
    z_up[0][0].start()
    z_down[0][0].start()
    for copy in cs_copies:
        copy.start()
    z_up[1][0].start()
    z_down[1][0].start()
    h_down.start()
    h_up.start()

    def weight_rows(r, carry):
        rows = pl.ds(pl.multiple_of(r * CELL, CELL), CELL)
        lane = lanes(CELL)
        for c in range(CPS // 2):
            cols = pl.ds(128 * c, 128)
            total = jnp.zeros((CELL, 128), f32)
            for v in range(2):
                left = cov[v, r * CPS + 2 * c].astype(f32)
                right = cov[v, r * CPS + 2 * c + 1].astype(f32)
                w = jnp.where(lane < CELL, left, right) / var[v, rows, cols]
                weight[v, rows, cols] = w
                total = total + w
            den[rows, cols] = total
        return carry

    lax.fori_loop(0, CPS, weight_rows, 0)
    den_copies = []
    for d in range(1, N_VERT):
        target = lax.rem(x + d, N_VERT)
        den_copies.append(
            remote(
                den.at[pl.ds(pl.multiple_of(target * SHARE, SHARE), SHARE)], rden.at[d],
                dsend.at[d], drecv.at[d], {"vert": target},
            )
        )
        den_copies[-1].start()

    for step in range(1, 4):
        for v in range(2):
            z_up[v][step - 1].wait_recv()
            z_up[v][step].start()
            if step < 3:
                z_down[v][step - 1].wait_recv()
                z_down[v][step].start()

    own_image.wait()
    h_down.wait_recv()
    h_up.wait_recv()

    @pl.when(a == 0)
    def _():
        ext[:, 0:BORDER, :] = jnp.zeros((2, BORDER, SIDE), f32)

    @pl.when(a == N_LINE - 1)
    def _():
        ext[:, BORDER + SIDE:ROWS, :] = jnp.zeros((2, BORDER, SIDE), f32)

    def pack(v, carry):
        lane = lanes(CHUNK)
        last = jnp.zeros((CHUNK, 128), f32)
        first = jnp.zeros((CHUNK, 128), f32)
        for g in range(ROWS // CHUNK):
            inside = (lane >= HALF * g) & (lane < HALF * (g + 1))
            rows = slice(CHUNK * g, CHUNK * (g + 1))
            last = jnp.where(inside, turn(ext[v, rows, 256:384], HALF * g - 108), last)
            first = jnp.where(inside, turn(ext[v, rows, 0:128], HALF * g), first)
        xs[0, v] = last
        xs[1, v] = first
        return carry

    lax.fori_loop(0, 2, pack, 0)
    x_copies = [
        remote(xs.at[0], xr.at[0], xsend.at[0], xrecv.at[0], at_px(1)),
        remote(xs.at[1], xr.at[1], xsend.at[1], xrecv.at[1], at_px(N_LINE - 1)),
    ]
    for copy in x_copies:
        copy.start()

    for copy in cs_copies:
        copy.wait_recv()
    names = csb[...].reshape(8 * N_LINE, 128)
    wanted = jnp.concatenate([names, names], axis=0).T
    lane = lax.broadcasted_iota(jnp.int32, (1, 384), 1)
    behind = jnp.zeros((1, 384), jnp.int32)
    for n in range(1, N_LINE):
        behind = behind + (lane >= PAD * n).astype(jnp.int32)
    slot = lane - PAD * behind
    owner = (a - behind + N_LINE) & (N_LINE - 1)
    stored = ((owner * N_LINE + b) * CELLS + slot).astype(f32)
    stored = jnp.where(slot < CELLS, stored, -2.0)

    s_copies = [[None] * N_LINE for _ in range(2)]
    for v in range(2):
        z_up[v][3].wait_recv()
        z_down[v][2].wait_recv()
        high, low = split(zbuf[v].reshape(N_LINE * PAD, 256))
        table = jnp.concatenate([high, low], axis=1)
        table = jnp.concatenate([table, jnp.zeros((384 - N_LINE * PAD, 512), bf16)], axis=0)
        hot = jnp.concatenate(
            [
                jnp.where(wanted[0:PAD, 8 * d + v:8 * d + v + 1] == stored, 1.0, 0.0)
                for d in range(N_LINE)
            ],
            axis=0,
        ).astype(bf16)
        picked = jnp.dot(hot, table, preferred_element_type=f32)
        sbuf[v] = (picked[:, 0:256] + picked[:, 256:512]).reshape(N_LINE, PAD, 256)
        for d in range(1, N_LINE):
            s_copies[v][d] = remote(
                sbuf.at[v, d], rbuf.at[v, N_LINE - d], ssend.at[v, d],
                srecv.at[v, N_LINE - d], at_px(d),
            )
            s_copies[v][d].start()

    for copy in x_copies:
        copy.wait_recv()

    def tiles(v, carry):
        tall = 2 * CHUNK
        lane = lanes(tall)
        for j in range(ROWS // tall):
            rows = slice(tall * j, tall * (j + 1))
            raw = [ext[v, rows, 128 * d:128 * (d + 1)] for d in range(3)]
            even = [turn(t, HALF) for t in raw]
            odd = [turn(t, 84) for t in raw]
            border = xr[0, v]
            left = jnp.concatenate(
                [turn(border, -HALF * g) for g in (2 * j, 2 * j + 1)], axis=0
            )
            left = jnp.where(b == 0, 0.0, left)
            border = xr[1, v]
            right = jnp.concatenate(
                [turn(border, 84 - HALF * g) for g in (2 * j, 2 * j + 1)], axis=0
            )
            right = jnp.where(b == N_LINE - 1, 0.0, right)
            before = [left] + even
            after = odd + [right]
            for d in range(3):
                high, low = split(jnp.where(lane < HALF, before[d], even[d]))
                thi[v, 2 * d, rows] = high
                tlo[v, 2 * d, rows] = low
                high, low = split(jnp.where(lane < 84, odd[d], after[d + 1]))
                thi[v, 2 * d + 1, rows] = high
                tlo[v, 2 * d + 1, rows] = low
        return carry

    lax.fori_loop(0, 2, tiles, 0)

    for v in range(2):
        for d in range(1, N_LINE):
            s_copies[v][d].wait_recv()
        total = sbuf[v, 0]
        for d in range(1, N_LINE):
            total = total + rbuf[v, d]
        for p in range(2 * RANK):
            tile = total[:, 128 * (p // 3):128 * (p // 3 + 1)]
            tap = jnp.where(lanes(PAD) < TAPS, turn(tile, -TAPS * (p % 3)), 0.0)
            high = tap.astype(bf16).astype(f32)
            taps[v, p, 0] = high
            taps[v, p, 1] = tap - high

    def band(v, p, part, q, count, shift):
        row = jnp.broadcast_to(taps[v, p, part, pl.ds(q, 1), :], (count, 128))
        return pltpu.roll(row, shift, 1, stride=1, stride_axis=0)

    def convolve(v, r, c, q):
        half = CELL // 2
        lane = lanes(half)
        row_bands = []
        for k in range(RANK):
            near = band(v, 2 * k, 0, q, half, 4)
            low = band(v, 2 * k, 1, q, half, WINDOW + 4)
            far = band(v, 2 * k, 0, q, half, 2 * WINDOW + 4 - 128)
            row_bands.append(
                jnp.concatenate(
                    [
                        jnp.where(lane < WINDOW, near, low),
                        jnp.where(lane < 2 * WINDOW - 128, low, far),
                    ],
                    axis=1,
                )
            )
        row_bands = jnp.concatenate(row_bands, axis=0).astype(bf16)
        top = pl.multiple_of(r * CELL, CELL)
        windows = []
        for h in range(2):
            rows = pl.ds(pl.multiple_of(top + half * h, half), WINDOW)
            high = thi[v, c, rows, :]
            windows.append(
                jnp.concatenate([high, high, tlo[v, c, rows, :], high[0:16]], axis=0)
            )
        window = jnp.concatenate(windows, axis=1)
        partial_pass = jnp.dot(row_bands, window, preferred_element_type=f32)
        high, low = split(partial_pass)
        left = jnp.concatenate(
            [
                jnp.concatenate(
                    [
                        part[half * k:half * (k + 1), 128 * h:128 * (h + 1)]
                        for k in range(RANK)
                    ],
                    axis=1,
                )
                for part in (high, low)
                for h in range(2)
            ],
            axis=0,
        )
        col_bands = jnp.concatenate(
            [
                jnp.concatenate(
                    [band(v, 2 * k + 1, part, q, CELL, 0) for k in range(RANK)], axis=1
                )
                for part in range(2)
            ],
            axis=0,
        ).astype(bf16)
        both = lax.dot_general(
            left, col_bands, (((1,), (1,)), ((), ())), preferred_element_type=f32
        )
        both = both[0:CELL] + both[CELL:2 * CELL]
        return both + turn(both, CELL)

    def num_copy(t):
        d = lax.rem(t - x + N_VERT, N_VERT)
        return d, remote(
            num.at[pl.ds(SHARE * t, SHARE)], rnum.at[d], nsend.at[t], nrecv.at[d], {"vert": t}
        )

    def cell_row(r, carry):
        rows = pl.ds(pl.multiple_of(r * CELL, CELL), CELL)

        def cell_pair(c, carry):
            cols = pl.ds(pl.multiple_of(c * 128, 128), 128)
            total = jnp.zeros((CELL, 128), f32)
            for v in range(2):
                q = r * CPS + 2 * c
                one = convolve(v, r, 2 * c, q)
                two = convolve(v, r, 2 * c + 1, q + 1)
                total = total + weight[v, rows, cols] * jnp.where(lanes(CELL) < CELL, one, two)
            num[rows, cols] = total
            return carry

        lax.fori_loop(0, CPS // 2, cell_pair, 0)
        for t, ready in enumerate((1, 2, 4, 5)):
            d, copy = num_copy(t)

            @pl.when((r == ready) & (d != 0))
            def _():
                copy.start()

        return carry

    lax.fori_loop(0, CPS, cell_row, 0)

    mine = pl.ds(pl.multiple_of(x * SHARE, SHARE), SHARE)
    for copy in den_copies:
        copy.wait_recv()
    total = den[mine]
    for d in range(1, N_VERT):
        total = total + rden[d]
    total = jnp.maximum(total, 0.5)
    wsum[...] = total
    upper = num[mine]
    for d in range(1, N_VERT):
        remote(rnum.at[d], rnum.at[d], nsend.at[0], nrecv.at[d], {"vert": lax.rem(x + 1, N_VERT)}).wait_recv()
        upper = upper + rnum[d]
    coadd[...] = upper / total

    for t in range(N_VERT):
        d, copy = num_copy(t)

        @pl.when(d != 0)
        def _():
            copy.wait_send()

    for copy in den_copies + cs_copies + x_copies + [h_down, h_up]:
        copy.wait_send()
    for v in range(2):
        for copy in z_up[v] + z_down[v] + s_copies[v][1:]:
            copy.wait_send()


def shards(warped_image, variance, kernel_factors, cell_source, coverage):
    vmem = pl.BlockSpec(memory_space=pltpu.VMEM)
    dma = pltpu.SemaphoreType.DMA
    out = jax.ShapeDtypeStruct((SHARE, SIDE), f32)
    return pl.pallas_call(
        kernel,
        out_shape=(out, out),
        in_specs=[
            pl.BlockSpec(memory_space=pl.ANY), vmem, vmem, vmem,
            pl.BlockSpec(memory_space=pltpu.SMEM),
        ],
        out_specs=(vmem, vmem),
        scratch_shapes=[
            pltpu.VMEM((2, ROWS, SIDE), f32),
            pltpu.VMEM((2, N_LINE, PAD, 256), f32),
            pltpu.VMEM((N_LINE, 8, 128), f32),
            pltpu.VMEM((2, N_LINE, PAD, 256), f32),
            pltpu.VMEM((2, N_LINE, PAD, 256), f32),
            pltpu.VMEM((2, 2 * RANK, 2, PAD, 128), f32),
            pltpu.VMEM((2, 2, CHUNK, 128), f32),
            pltpu.VMEM((2, 2, CHUNK, 128), f32),
            pltpu.VMEM((2, CPS, ROWS, 128), bf16),
            pltpu.VMEM((2, CPS, ROWS, 128), bf16),
            pltpu.VMEM((2, SIDE, SIDE), f32),
            pltpu.VMEM((SIDE, SIDE), f32),
            pltpu.VMEM((SIDE, SIDE), f32),
            pltpu.VMEM((N_VERT, SHARE, SIDE), f32),
            pltpu.VMEM((N_VERT, SHARE, SIDE), f32),
            dma,
            dma((2, N_LINE)), dma((2, N_LINE)),
            dma((N_LINE,)), dma((N_LINE,)),
            dma((2, N_LINE)), dma((2, N_LINE)),
            dma((2,)), dma((2,)), dma((2,)), dma((2,)),
            dma((N_VERT,)), dma((N_VERT,)), dma((N_VERT,)), dma((N_VERT,)),
        ],
        compiler_params=pltpu.CompilerParams(
            collective_id=0, has_side_effects=True, vmem_limit_bytes=40 * 1024 * 1024
        ),
    )(warped_image, variance, kernel_factors, cell_source, coverage)


def solution(mesh):
    placed = (
        P("vert", "py", "px"),
        P("vert", "py", "px"),
        P("vert", ("py", "px"), None),
        P("vert", ("py", "px")),
        P("vert", ("py", "px")),
    )
    return jax.shard_map(
        shards,
        mesh=mesh,
        in_specs=placed,
        out_specs=(P(("py", "vert"), "px"), P(("py", "vert"), "px")),
        check_vma=False,
    )
```

time: 196 us -> 62.6 us (0.32)
  waiting for transfers between devices: 102 us -> 0 us
  Pallas kernels: 0 us -> 55.4 us
  local copies, waits for them, and re-layouts: 34 us -> 6.11 us
  matrix products: 25.3 us -> 0 us
  between operations: 14.4 us -> 0.64 us
  starting transfers between devices: 12.1 us -> 0 us
  other arithmetic: 7.98 us -> 0 us
    pallas_call x0 -> x1, Pallas kernels: none -> 55.4 us  [shards(): pl.pallas_call(kernel, out_shape=(out, out), in_specs=[pl.BlockSpec(memor...]
    psum x1 -> x0, waiting for transfers between devices: 47.7 us -> none  [shards(): lax.psum((numerator_term, denominator_term), 'vert')]
    all_gather x1 -> x0, waiting for transfers between devices: 44.8 us -> none  [shards(): lax.all_gather(kernel_factors, ('py', 'px'), axis=1, tiled=True)]
    dot_general x8 -> x0, matrix products: 25.3 us -> none  [the longest x2 9.62 us: convolve_cells(): jnp.einsum('cril,crjl->cij', partial_pass, col_bands, precision=highest)]
    slice x13 -> x0, local copies, waits for them, and re-layouts: 13 us -> none  [the longest x4 7.05 us: cell_windows(): stripes[:, :, CELL:width + CELL]]
    ppermute x4 -> x0, starting transfers between devices: 12 us -> none  [the longest x2 8.82 us: with_halo(): lax.ppermute(lax.slice_in_dim(block, block.shape[dim] - width, None, axis...]
    ppermute x4 -> x0, waiting for transfers between devices: 8.49 us -> none  [the longest x2 4.9 us: with_halo(): lax.ppermute(lax.slice_in_dim(block, 0, width, axis=dim), axis, backward)]
    another operation x6 -> x0, local copies, waits for them, and re-layouts: 6.04 us -> none  [the longest x4 4.99 us: shards(): convolved = jnp.stack(convolved_list)]
  transfers between devices with their start and end apart: 6 -> 0, of which waited for: 4 -> 0; matrix products, arithmetic and copies ran while one was open for 11% -> 0% of each run, Pallas kernels for 0% -> 0%
where the time goes in v1:
time: 62.6 us; the launch traced here: 62.1 us
  Pallas kernels  55.4 us (88%)
  local copies, waits for them, and re-layouts  6.11 us (10%)
  between operations  0.64 us (1%)
    pallas_call x1, Pallas kernels, shards(): pl.pallas_call(kernel, out_shape=(out, out), in_specs=[pl.BlockSpec(memor...  55.4 us
    unnamed x11, local copies, waits for them, and re-layouts  6.11 us

profile of v1, /device:TPU:1, one launch (start us, length us, event | category | flops | bytes accessed | tf_op | source)
XLA Modules:
  0.0 62.1 jit_solution(1344346973147255718)
XLA Ops:
  0.6 0.9 %copy.7.fac = f32[2,36,246]{2,1,0:T(8,128)S(1)} copy(f32[2,36,246]{2,0,1:T(2,128)} %param.7) | data formatting | bytes 141696 | tf_op args[2]
  1.5 0.0 copy-start
  1.5 1.3 %copy-done = f32[2,384,384]{2,1,0:T(8,128)S(1)} copy-done((f32[2,384,384]{2,1,0:T(8,128)S(1)}, f32[2,384,384]{2,1,0:T(8,128)}, u32[]{:S(2)}) %copy-start) | copy-done | bytes 1179672
  2.8 0.0 copy-start.1
  2.8 1.3 %copy-done.1 = f32[2,384,384]{2,1,0:T(8,128)S(1)} copy-done((f32[2,384,384]{2,1,0:T(8,128)S(1)}, f32[2,384,384]{2,1,0:T(8,128)}, u32[]{:S(2)}) %copy-start.1) | copy-done | bytes 1179672
  4.1 0.0 copy-start.2
  4.1 0.7 %copy-done.2 = s32[2,36]{1,0:T(2,128)S(1)} copy-done((s32[2,36]{1,0:T(2,128)S(1)}, s32[2,36]{1,0:T(2,128)}, u32[]{:S(2)}) %copy-start.2) | copy-done | bytes 312
  4.7 0.0 copy-start.3
  4.7 0.7 %copy-done.3 = s32[2,36]{1,0:T(2,128)S(1)} copy-done((s32[2,36]{1,0:T(2,128)S(1)}, s32[2,36]{1,0:T(2,128)}, u32[]{:S(2)}) %copy-start.3) | copy-done | bytes 312
  5.4 55.4 %shard_map.68 = (f32[96,384]{1,0:T(8,128)S(1)}, f32[96,384]{1,0:T(8,128)S(1)}) custom-call(f32[2,384,384]{2,1,0:T(8,128)S(1)} %copy-done, f32[2,384,384]{2,1,0:T(8,128)S(1)} %copy-done.1, f32[2,36,246]{2,1,0:T(8,128)S(1)} %copy.7.fac, s32[2,36]{1,0:T(2,128)S(1)} %copy-done.2, s32[2,36]{1,0:T(2,128)S(1)} %copy-done.3), custom_call_target="tpu_custom_call" | custom-call | tf_op jit(solution)/shard_map/pallas_call | solution.py:401
  60.8 0.7 %copy.10 = f32[96,384]{1,0:T(8,128)} copy(f32[96,384]{1,0:T(8,128)S(1)} %get-tuple-element.4) | data formatting | bytes 294912
  61.5 0.7 %copy.11 = f32[96,384]{1,0:T(8,128)} copy(f32[96,384]{1,0:T(8,128)S(1)} %get-tuple-element.5) | data formatting | bytes 294912
Async XLA Ops:
  1.5 1.3 %copy-start = (f32[2,384,384]{2,1,0:T(8,128)S(1)}, f32[2,384,384]{2,1,0:T(8,128)}, u32[]{:S(2)}) copy-start(f32[2,384,384]{2,1,0:T(8,128)} %img.1) | copy-start | bytes 3538948
  2.8 1.3 %copy-start.1 = (f32[2,384,384]{2,1,0:T(8,128)S(1)}, f32[2,384,384]{2,1,0:T(8,128)}, u32[]{:S(2)}) copy-start(f32[2,384,384]{2,1,0:T(8,128)} %var.1) | copy-start | bytes 3538948
  4.1 0.7 %copy-start.2 = (s32[2,36]{1,0:T(2,128)S(1)}, s32[2,36]{1,0:T(2,128)}, u32[]{:S(2)}) copy-start(s32[2,36]{1,0:T(2,128)} %cs.1) | copy-start | bytes 868
  4.7 0.7 %copy-start.3 = (s32[2,36]{1,0:T(2,128)S(1)}, s32[2,36]{1,0:T(2,128)}, u32[]{:S(2)}) copy-start(s32[2,36]{1,0:T(2,128)} %cov.1) | copy-start | bytes 868

commit v2 on v1

v2 whole, which is shorter than its diff:
```python
import jax
import jax.numpy as jnp
from jax import lax
from jax.experimental import pallas as pl
from jax.experimental.pallas import tpu as pltpu
from jax.sharding import PartitionSpec as P

TAPS = 41
RANK = 3
CELL = 64
HALF = 20
CPS = 6
SIDE = 384
CELLS = 36
PAD = 40
FACT = 246
BORDER = 24
ROWS = SIDE + 2 * BORDER
WINDOW = 80
SHARE = 96
CHUNK = 72
N_VERT = 4
N_LINE = 8

MESH = pl.DeviceIdType.MESH
f32 = jnp.float32
bf16 = jnp.bfloat16


def lanes(rows):
    return lax.broadcasted_iota(jnp.int32, (rows, 128), 1)


def turn(x, shift):
    shift = shift % 128
    return x if shift == 0 else pltpu.roll(x, shift, 1)


def split(x):
    high = x.astype(bf16)
    low = (x - high.astype(f32)).astype(bf16)
    return high, low


def kernel(
    img, var_in, fac_in, cs_in, cov_in,
    top_sum, weight_sum,
    ext, var, fac, cs, cov, zbuf, csb, hot, sbuf, rbuf, taps, xs, xr, thi, tlo, weight, num, den,
    rnum, rden, halves,
    in_sem, zsend, zrecv, csend, crecv, ssend, srecv, hsend, hrecv, xsend, xrecv,
    nsend, nrecv, dsend, drecv,
):
    a = lax.axis_index("py")
    b = lax.axis_index("px")
    x = lax.axis_index("vert")
    others = (lax.rem(x + 2, N_VERT), N_VERT - 1 - x, x + 1 - 2 * lax.rem(x, 2))

    def at_py(d):
        return {"py": lax.rem(a + d, N_LINE)}

    def at_px(d):
        return {"px": lax.rem(b + d, N_LINE)}

    def remote(src, dst, send, recv, device):
        return pltpu.make_async_remote_copy(
            src_ref=src, dst_ref=dst, send_sem=send, recv_sem=recv,
            device_id=device, device_id_type=MESH,
        )

    barrier = pltpu.get_barrier_semaphore()
    for d in range(1, N_LINE):
        pl.semaphore_signal(barrier, inc=1, device_id=at_py(d), device_id_type=MESH)
    for d in range(1, N_LINE):
        pl.semaphore_signal(barrier, inc=1, device_id=at_px(d), device_id_type=MESH)
    for target in others:
        pl.semaphore_signal(barrier, inc=1, device_id={"vert": target}, device_id_type=MESH)

    inputs = [
        pltpu.make_async_copy(source, target, in_sem.at[n])
        for n, (source, target) in enumerate((
            (fac_in, fac), (cs_in, cs), (cov_in, cov), (var_in, var),
            (img, ext.at[:, pl.ds(BORDER, SIDE), :]),
        ))
    ]
    for copy in inputs:
        copy.start()

    inputs[0].wait()
    for v in range(2):
        zbuf[v, 0] = jnp.zeros((PAD, 256), f32)
        zbuf[v, 0, 0:CELLS, 0:FACT] = fac[:, v, :]
    inputs[1].wait()
    csb[0] = jnp.full((8, 128), -1.0, f32)
    csb[0, 0:2, 0:CELLS] = cs[...].astype(f32)

    pl.semaphore_wait(barrier, 2 * (N_LINE - 1) + N_VERT - 1)

    def ring(v, source, target, d):
        return remote(
            zbuf.at[v, source], zbuf.at[v, target], zsend.at[v, target], zrecv.at[v, target],
            at_py(d),
        )

    z_first = [ring(0, 0, d, d) for d in (4, 3, 5, 2, 6, 1, 7)]
    z_up = [ring(1, s, t, 1) for s, t in ((0, 1), (1, 2), (2, 3), (3, 4))]
    z_down = [ring(1, s, t, N_LINE - 1) for s, t in ((0, 7), (7, 6), (6, 5))]
    cs_copies = [
        remote(csb.at[0], csb.at[N_LINE - d], csend.at[d], crecv.at[N_LINE - d], at_px(d))
        for d in range(1, N_LINE)
    ]
    h_down = remote(
        img.at[:, pl.ds(SIDE - BORDER, BORDER), :], ext.at[:, pl.ds(0, BORDER), :],
        hsend.at[0], hrecv.at[0], at_py(1),
    )
    h_up = remote(
        img.at[:, pl.ds(0, BORDER), :], ext.at[:, pl.ds(BORDER + SIDE, BORDER), :],
        hsend.at[1], hrecv.at[1], at_py(N_LINE - 1),
    )
    z_up[0].start()
    z_down[0].start()
    for copy in z_first + cs_copies + [h_down, h_up]:
        copy.start()

    def pass_on(step):
        z_up[step - 1].wait_recv()
        z_up[step].start()
        if step < 3:
            z_down[step - 1].wait_recv()
            z_down[step].start()

    inputs[2].wait()
    inputs[3].wait()

    def weight_rows(r, carry):
        rows = pl.ds(pl.multiple_of(r * CELL, CELL), CELL)
        lane = lanes(CELL)
        for c in range(CPS // 2):
            cols = pl.ds(128 * c, 128)
            total = jnp.zeros((CELL, 128), f32)
            for v in range(2):
                left = cov[v, r * CPS + 2 * c].astype(f32)
                right = cov[v, r * CPS + 2 * c + 1].astype(f32)
                w = jnp.where(lane < CELL, left, right) / var[v, rows, cols]
                weight[v, rows, cols] = w
                total = total + w
            den[rows, cols] = total
        return carry

    lax.fori_loop(0, CPS, weight_rows, 0)

    def share(ref, t):
        return ref.at[pl.ds(pl.multiple_of(t * SHARE, SHARE), SHARE)]

    den_copies = [
        remote(share(den, t), rden.at[n], dsend.at[n], drecv.at[n], {"vert": t})
        for n, t in enumerate(others)
    ]
    num_copies = [
        remote(share(num, t), rnum.at[n], nsend.at[n], nrecv.at[n], {"vert": t})
        for n, t in enumerate(others)
    ]
    for copy in den_copies:
        copy.start()
    pass_on(1)

    inputs[4].wait()
    h_down.wait_recv()
    h_up.wait_recv()

    @pl.when(a == 0)
    def _():
        ext[:, 0:BORDER, :] = jnp.zeros((2, BORDER, SIDE), f32)

    @pl.when(a == N_LINE - 1)
    def _():
        ext[:, BORDER + SIDE:ROWS, :] = jnp.zeros((2, BORDER, SIDE), f32)

    def pack(v, carry):
        lane = lanes(CHUNK)
        last = jnp.zeros((CHUNK, 128), f32)
        first = jnp.zeros((CHUNK, 128), f32)
        for g in range(ROWS // CHUNK):
            inside = (lane >= HALF * g) & (lane < HALF * (g + 1))
            rows = slice(CHUNK * g, CHUNK * (g + 1))
            last = jnp.where(inside, turn(ext[v, rows, 256:384], HALF * g - 108), last)
            first = jnp.where(inside, turn(ext[v, rows, 0:128], HALF * g), first)
        xs[0, v] = last
        xs[1, v] = first
        return carry

    lax.fori_loop(0, 2, pack, 0)
    x_copies = [
        remote(xs.at[0], xr.at[0], xsend.at[0], xrecv.at[0], at_px(1)),
        remote(xs.at[1], xr.at[1], xsend.at[1], xrecv.at[1], at_px(N_LINE - 1)),
    ]
    for copy in x_copies:
        copy.start()

    for copy in cs_copies:
        copy.wait_recv()
    names = csb[...].reshape(8 * N_LINE, 128)
    wanted = jnp.concatenate([names, names], axis=0).T
    lane = lax.broadcasted_iota(jnp.int32, (1, 384), 1)
    behind = jnp.zeros((1, 384), jnp.int32)
    for n in range(1, N_LINE):
        behind = behind + (lane >= PAD * n).astype(jnp.int32)
    slot = lane - PAD * behind
    owner = (a - behind + N_LINE) & (N_LINE - 1)
    stored = ((owner * N_LINE + b) * CELLS + slot).astype(f32)
    stored = jnp.where(slot < CELLS, stored, -2.0)
    for v in range(2):
        hot[v] = jnp.concatenate(
            [
                jnp.where(wanted[0:PAD, 8 * d + v:8 * d + v + 1] == stored, 1.0, 0.0)
                for d in range(N_LINE)
            ],
            axis=0,
        ).astype(bf16)
    pass_on(2)

    for copy in x_copies:
        copy.wait_recv()

    def tiles(v, carry):
        tall = 2 * CHUNK
        lane = lanes(tall)
        for j in range(ROWS // tall):
            rows = slice(tall * j, tall * (j + 1))
            raw = [ext[v, rows, 128 * d:128 * (d + 1)] for d in range(3)]
            even = [turn(t, HALF) for t in raw]
            odd = [turn(t, 84) for t in raw]
            border = xr[0, v]
            left = jnp.concatenate(
                [turn(border, -HALF * g) for g in (2 * j, 2 * j + 1)], axis=0
            )
            left = jnp.where(b == 0, 0.0, left)
            border = xr[1, v]
            right = jnp.concatenate(
                [turn(border, 84 - HALF * g) for g in (2 * j, 2 * j + 1)], axis=0
            )
            right = jnp.where(b == N_LINE - 1, 0.0, right)
            before = [left] + even
            after = odd + [right]
            for d in range(3):
                high, low = split(jnp.where(lane < HALF, before[d], even[d]))
                thi[v, 2 * d, rows] = high
                tlo[v, 2 * d, rows] = low
                high, low = split(jnp.where(lane < 84, odd[d], after[d + 1]))
                thi[v, 2 * d + 1, rows] = high
                tlo[v, 2 * d + 1, rows] = low
        return carry

    lax.fori_loop(0, 2, tiles, 0)
    pass_on(3)

    s_copies = [
        [
            remote(
                sbuf.at[v, d], rbuf.at[v, N_LINE - d], ssend.at[v, d],
                srecv.at[v, N_LINE - d], at_px(d),
            )
            for d in range(1, N_LINE)
        ]
        for v in range(2)
    ]
    for v, arrivals in ((0, z_first), (1, [z_up[3], z_down[2]])):
        for copy in arrivals:
            copy.wait_recv()
        high, low = split(zbuf[v].reshape(N_LINE * PAD, 256))
        table = jnp.concatenate([high, low], axis=1)
        table = jnp.concatenate([table, jnp.zeros((384 - N_LINE * PAD, 512), bf16)], axis=0)
        picked = jnp.dot(hot[v], table, preferred_element_type=f32)
        sbuf[v] = (picked[:, 0:256] + picked[:, 256:512]).reshape(N_LINE, PAD, 256)
        for copy in s_copies[v]:
            copy.start()

    half = CELL // 2

    def receive_taps(v):
        for copy in s_copies[v]:
            copy.wait_recv()
        total = sbuf[v, 0]
        for d in range(1, N_LINE):
            total = total + rbuf[v, d]
        lane = lanes(PAD)
        for p in range(2 * RANK):
            n, offset = divmod(TAPS * p, 128)
            tap = turn(total[:, 128 * n:128 * (n + 1)], -offset)
            if offset + TAPS > 128:
                rest = turn(total[:, 128 * (n + 1):128 * (n + 2)], -offset)
                tap = jnp.where(lane < 128 - offset, tap, rest)
            tap = jnp.where(lane < TAPS, tap, 0.0)
            high = tap.astype(bf16).astype(f32)
            taps[v, p, 0] = high
            taps[v, p, 1] = tap - high

    def band(v, p, part, q, count, shift):
        row = jnp.broadcast_to(taps[v, p, part, pl.ds(q, 1), :], (count, 128))
        return pltpu.roll(row, shift, 1, stride=1, stride_axis=0)

    def row_bands(v, q):
        lane = lanes(half)
        parts = []
        for k in range(RANK):
            near = band(v, 2 * k, 0, q, half, 4)
            low = band(v, 2 * k, 1, q, half, WINDOW + 4)
            far = band(v, 2 * k, 0, q, half, 2 * WINDOW + 4 - 128)
            parts.append(
                jnp.concatenate(
                    [
                        jnp.where(lane < WINDOW, near, low),
                        jnp.where(lane < 2 * WINDOW - 128, low, far),
                    ],
                    axis=1,
                )
            )
        return jnp.concatenate(parts, axis=0).astype(bf16)

    def col_bands(v, q):
        return jnp.concatenate(
            [
                jnp.concatenate(
                    [band(v, 2 * k + 1, part, q, CELL, 0) for k in range(RANK)], axis=1
                )
                for part in range(2)
            ],
            axis=0,
        ).astype(bf16)

    def row_of(step):
        late = step // 3
        place = step - 3 * late
        flip = lax.rem(x + late, 2)
        place = place + flip * (2 - 2 * place)
        side = x // 2
        return 3 * ((1 - side) * (1 - late) + side * late) + place

    def row_pass(v, step):
        r = row_of(step)
        top = pl.multiple_of(r * CELL, CELL)
        for c in range(CPS):
            windows = []
            for h in range(2):
                rows = pl.ds(pl.multiple_of(top + half * h, half), WINDOW)
                high = thi[v, c, rows, :]
                windows.append(
                    jnp.concatenate([high, high, tlo[v, c, rows, :], high[0:16]], axis=0)
                )
            part = jnp.dot(
                row_bands(v, r * CPS + c), jnp.concatenate(windows, axis=1),
                preferred_element_type=f32,
            )
            halves[lax.rem(step, 2) * CPS + c] = jnp.concatenate(
                [
                    jnp.concatenate(
                        [
                            piece[half * k:half * (k + 1), 128 * h:128 * (h + 1)]
                            for k in range(RANK)
                        ],
                        axis=1,
                    )
                    for piece in split(part)
                    for h in range(2)
                ],
                axis=0,
            )

    def col_pass(v, step):
        r = row_of(step)
        rows = pl.ds(pl.multiple_of(r * CELL, CELL), CELL)
        for c in range(0, CPS, 2):
            pair = []
            for n in (c, c + 1):
                both = lax.dot_general(
                    halves[lax.rem(step, 2) * CPS + n], col_bands(v, r * CPS + n),
                    (((1,), (1,)), ((), ())), preferred_element_type=f32,
                )
                both = both[0:CELL] + both[CELL:2 * CELL]
                pair.append(both + turn(both, CELL))
            cols = slice(CELL * c, CELL * c + 128)
            term = weight[v, rows, cols] * jnp.where(lanes(CELL) < CELL, pair[0], pair[1])
            num[rows, cols] = term if v == 0 else num[rows, cols] + term

    for v in range(2):
        receive_taps(v)
        row_pass(v, jnp.int32(0))

        def cell_row(step, carry):
            row_pass(v, step)
            col_pass(v, step - 1)
            if v == 1:
                for n, ready in enumerate((2, 3, 5)):

                    @pl.when(step == ready)
                    def _():
                        num_copies[n].start()

            return carry

        lax.fori_loop(1, CPS, cell_row, 0)
        col_pass(v, jnp.int32(CPS - 1))

    mine = pl.ds(pl.multiple_of(x * SHARE, SHARE), SHARE)
    for copy in den_copies + num_copies:
        copy.wait_recv()
    weight_sum[...] = (den[mine] + rden[1]) + (rden[0] + rden[2])
    top_sum[...] = (num[mine] + rnum[1]) + (rnum[0] + rnum[2])

    for copy in z_first + z_up + z_down + cs_copies + [h_down, h_up] + x_copies:
        copy.wait_send()
    for copy in s_copies[0] + s_copies[1] + den_copies + num_copies:
        copy.wait_send()


def shards(warped_image, variance, kernel_factors, cell_source, coverage):
    vmem = pl.BlockSpec(memory_space=pltpu.VMEM)
    dma = pltpu.SemaphoreType.DMA
    out = jax.ShapeDtypeStruct((SHARE, SIDE), f32)
    top_sum, weight_sum = pl.pallas_call(
        kernel,
        out_shape=(out, out),
        in_specs=[pl.BlockSpec(memory_space=pl.ANY)] * 5,
        out_specs=(vmem, vmem),
        scratch_shapes=[
            pltpu.VMEM((2, ROWS, SIDE), f32),
            pltpu.VMEM((2, SIDE, SIDE), f32),
            pltpu.VMEM((CELLS, 2, FACT), f32),
            pltpu.VMEM((2, CELLS), jnp.int32),
            pltpu.SMEM((2, CELLS), jnp.int32),
            pltpu.VMEM((2, N_LINE, PAD, 256), f32),
            pltpu.VMEM((N_LINE, 8, 128), f32),
            pltpu.VMEM((2, N_LINE * PAD, 384), bf16),
            pltpu.VMEM((2, N_LINE, PAD, 256), f32),
            pltpu.VMEM((2, N_LINE, PAD, 256), f32),
            pltpu.VMEM((2, 2 * RANK, 2, PAD, 128), f32),
            pltpu.VMEM((2, 2, CHUNK, 128), f32),
            pltpu.VMEM((2, 2, CHUNK, 128), f32),
            pltpu.VMEM((2, CPS, ROWS, 128), bf16),
            pltpu.VMEM((2, CPS, ROWS, 128), bf16),
            pltpu.VMEM((2, SIDE, SIDE), f32),
            pltpu.VMEM((SIDE, SIDE), f32),
            pltpu.VMEM((SIDE, SIDE), f32),
            pltpu.VMEM((N_VERT - 1, SHARE, SIDE), f32),
            pltpu.VMEM((N_VERT - 1, SHARE, SIDE), f32),
            pltpu.VMEM((2 * CPS, 128, 384), bf16),
            dma((5,)),
            dma((2, N_LINE)), dma((2, N_LINE)),
            dma((N_LINE,)), dma((N_LINE,)),
            dma((2, N_LINE)), dma((2, N_LINE)),
            dma((2,)), dma((2,)), dma((2,)), dma((2,)),
            dma((3,)), dma((3,)), dma((3,)), dma((3,)),
        ],
        compiler_params=pltpu.CompilerParams(
            collective_id=0, has_side_effects=True, vmem_limit_bytes=60 * 1024 * 1024
        ),
    )(warped_image, variance, kernel_factors.transpose(1, 0, 2), cell_source, coverage)
    weight_sum = jnp.maximum(weight_sum, 0.5)
    return top_sum / weight_sum, weight_sum


def solution(mesh):
    placed = (
        P("vert", "py", "px"),
        P("vert", "py", "px"),
        P("vert", ("py", "px"), None),
        P("vert", ("py", "px")),
        P("vert", ("py", "px")),
    )
    return jax.shard_map(
        shards,
        mesh=mesh,
        in_specs=placed,
        out_specs=(P(("py", "vert"), "px"), P(("py", "vert"), "px")),
        check_vma=False,
    )
```

time: 62.6 us -> 54.2 us (0.87)
  local copies, waits for them, and re-layouts: 6.11 us -> 0 us
  Pallas kernels: 55.4 us -> 51.7 us
  other arithmetic: 0 us -> 1.71 us
    unnamed x11 -> x0, local copies, waits for them, and re-layouts: 6.11 us -> none
    pallas_call x1, Pallas kernels: 55.4 us -> 51.7 us  [shards(): pl.pallas_call(kernel, out_shape=(out, out), in_specs=[pl.BlockSpec(memor...]
    div x0 -> x1, other arithmetic: none -> 1.71 us  [shards(): return (top_sum / weight_sum, weight_sum)]
where the time goes in v2:
time: 54.2 us; the launch traced here: 54.1 us
  Pallas kernels  51.7 us (95%)
  other arithmetic  1.71 us (3%)
  between operations  0.64 us (1%)
    pallas_call x1, Pallas kernels, shards(): pl.pallas_call(kernel, out_shape=(out, out), in_specs=[pl.BlockSpec(memor...  51.7 us
    div x1, other arithmetic, shards(): return (top_sum / weight_sum, weight_sum)  1.71 us

profile of v2, /device:TPU:1, one launch (start us, length us, event | category | flops | bytes accessed | tf_op | source)
XLA Modules:
  0.0 54.1 jit_solution(15874863129636885995)
XLA Ops:
  0.6 51.7 %shard_map.68 = (f32[96,384]{1,0:T(8,128)}, f32[96,384]{1,0:T(8,128)}) custom-call(f32[2,384,384]{2,1,0:T(8,128)} %img.1, f32[2,384,384]{2,1,0:T(8,128)} %var_in.1, f32[36,2,246]{2,1,0:T(2,128)} %bitcast.1, s32[2,36]{1,0:T(2,128)} %cs_in.1, s32[2,36]{1,0:T(2,128)} %cov_in.1), custom_call_target="tpu_custom_call" | custom-call | tf_op jit(solution)/shard_map/pallas_call | solution.py:419
  52.4 1.7 %fusion = (f32[96,384]{1,0:T(8,128)}, f32[96,384]{1,0:T(8,128)}) fusion(f32[96,384]{1,0:T(8,128)} %get-tuple-element.4, f32[96,384]{1,0:T(8,128)} %get-tuple-element.5), kind=kLoop, calls=%fused_computation.1 | loop fusion | flops 73728 | bytes 589824 | tf_op jit(solution)/shard_map/div | solution.py:458

commit v3 on v2

--- a/solution.py
+++ b/solution.py
@@ -18,6 +18,7 @@
 ROWS = SIDE + 2 * BORDER
 WINDOW = 80
 SHARE = 96
+EARLY = 16
 CHUNK = 72
 N_VERT = 4
 N_LINE = 8
@@ -116,9 +117,7 @@
         img.at[:, pl.ds(0, BORDER), :], ext.at[:, pl.ds(BORDER + SIDE, BORDER), :],
         hsend.at[1], hrecv.at[1], at_py(N_LINE - 1),
     )
-    z_up[0].start()
-    z_down[0].start()
-    for copy in z_first + cs_copies + [h_down, h_up]:
+    for copy in [h_down, h_up] + z_first + cs_copies + [z_up[0], z_down[0]]:
         copy.start()
 
     def pass_on(step):
@@ -155,13 +154,18 @@
         remote(share(den, t), rden.at[n], dsend.at[n], drecv.at[n], {"vert": t})
         for n, t in enumerate(others)
     ]
-    num_copies = [
-        remote(share(num, t), rnum.at[n], nsend.at[n], nrecv.at[n], {"vert": t})
-        for n, t in enumerate(others)
-    ]
     for copy in den_copies:
         copy.start()
-    pass_on(1)
+
+    def share_part(n, first, count, sem):
+        t = others[n]
+        first = first + lax.rem(t, 2) * (SHARE - count - 2 * first)
+        first = pl.multiple_of(first, 32)
+        base = pl.multiple_of(t * SHARE + first, 32)
+        return remote(
+            num.at[pl.ds(base, count)], rnum.at[n, pl.ds(first, count)],
+            nsend.at[sem], nrecv.at[sem], {"vert": t},
+        )
 
     inputs[4].wait()
     h_down.wait_recv()
@@ -195,6 +199,8 @@
     ]
     for copy in x_copies:
         copy.start()
+
+    pass_on(1)
 
     for copy in cs_copies:
         copy.wait_recv()
@@ -218,10 +224,36 @@
         ).astype(bf16)
     pass_on(2)
 
+    def pick_copies(v, first, count, sem):
+        rows = pl.ds(first, count)
+        return [
+            remote(
+                sbuf.at[v, d, rows], rbuf.at[v, N_LINE - d, rows], ssend.at[sem, d],
+                srecv.at[sem, N_LINE - d], at_px(d),
+            )
+            for d in range(1, N_LINE)
+        ]
+
+    s_copies = [pick_copies(0, 0, EARLY, 0), pick_copies(0, EARLY, PAD - EARLY, 1), pick_copies(1, 0, PAD, 2)]
+
+    def pick(v):
+        high, low = split(zbuf[v].reshape(N_LINE * PAD, 256))
+        table = jnp.concatenate([high, low], axis=1)
+        table = jnp.concatenate([table, jnp.zeros((384 - N_LINE * PAD, 512), bf16)], axis=0)
+        picked = jnp.dot(hot[v], table, preferred_element_type=f32)
+        sbuf[v] = (picked[:, 0:256] + picked[:, 256:512]).reshape(N_LINE, PAD, 256)
+
+    for copy in z_first:
+        copy.wait_recv()
+    pick(0)
+    for copy in s_copies[0] + s_copies[1]:
+        copy.start()
+    pass_on(3)
+
     for copy in x_copies:
         copy.wait_recv()
 
-    def tiles(v, carry):
+    def tiles(v):
         tall = 2 * CHUNK
         lane = lanes(tall)
         for j in range(ROWS // tall):
@@ -248,41 +280,26 @@
                 high, low = split(jnp.where(lane < 84, odd[d], after[d + 1]))
                 thi[v, 2 * d + 1, rows] = high
                 tlo[v, 2 * d + 1, rows] = low
-        return carry
-
-    lax.fori_loop(0, 2, tiles, 0)
-    pass_on(3)
-
-    s_copies = [
-        [
-            remote(
-                sbuf.at[v, d], rbuf.at[v, N_LINE - d], ssend.at[v, d],
-                srecv.at[v, N_LINE - d], at_px(d),
-            )
-            for d in range(1, N_LINE)
-        ]
-        for v in range(2)
-    ]
-    for v, arrivals in ((0, z_first), (1, [z_up[3], z_down[2]])):
-        for copy in arrivals:
+
+    tiles(0)
+    tiles(1)
+
+    for copy in (z_up[3], z_down[2]):
+        copy.wait_recv()
+    pick(1)
+    for copy in s_copies[2]:
+        copy.start()
+
+    half = CELL // 2
+
+    def receive_taps(v, first, count, copies):
+        for copy in copies:
             copy.wait_recv()
-        high, low = split(zbuf[v].reshape(N_LINE * PAD, 256))
-        table = jnp.concatenate([high, low], axis=1)
-        table = jnp.concatenate([table, jnp.zeros((384 - N_LINE * PAD, 512), bf16)], axis=0)
-        picked = jnp.dot(hot[v], table, preferred_element_type=f32)
-        sbuf[v] = (picked[:, 0:256] + picked[:, 256:512]).reshape(N_LINE, PAD, 256)
-        for copy in s_copies[v]:
-            copy.start()
-
-    half = CELL // 2
-
-    def receive_taps(v):
-        for copy in s_copies[v]:
-            copy.wait_recv()
-        total = sbuf[v, 0]
+        rows = slice(first, first + count)
+        total = sbuf[v, 0, rows]
         for d in range(1, N_LINE):
-            total = total + rbuf[v, d]
-        lane = lanes(PAD)
+            total = total + rbuf[v, d, rows]
+        lane = lanes(count)
         for p in range(2 * RANK):
             n, offset = divmod(TAPS * p, 128)
             tap = turn(total[:, 128 * n:128 * (n + 1)], -offset)
@@ -291,8 +308,8 @@
                 tap = jnp.where(lane < 128 - offset, tap, rest)
             tap = jnp.where(lane < TAPS, tap, 0.0)
             high = tap.astype(bf16).astype(f32)
-            taps[v, p, 0] = high
-            taps[v, p, 1] = tap - high
+            taps[v, p, 0, rows] = high
+            taps[v, p, 1, rows] = tap - high
 
     def band(v, p, part, q, count, shift):
         row = jnp.broadcast_to(taps[v, p, part, pl.ds(q, 1), :], (count, 128))
@@ -327,7 +344,9 @@
             axis=0,
         ).astype(bf16)
 
-    def row_of(step):
+    def row_of(v, step):
+        if v == 0:
+            return step
         late = step // 3
         place = step - 3 * late
         flip = lax.rem(x + late, 2)
@@ -336,7 +355,7 @@
         return 3 * ((1 - side) * (1 - late) + side * late) + place
 
     def row_pass(v, step):
-        r = row_of(step)
+        r = row_of(v, step)
         top = pl.multiple_of(r * CELL, CELL)
         for c in range(CPS):
             windows = []
@@ -366,7 +385,7 @@
             )
 
     def col_pass(v, step):
-        r = row_of(step)
+        r = row_of(v, step)
         rows = pl.ds(pl.multiple_of(r * CELL, CELL), CELL)
         for c in range(0, CPS, 2):
             pair = []
@@ -381,24 +400,42 @@
             term = weight[v, rows, cols] * jnp.where(lanes(CELL) < CELL, pair[0], pair[1])
             num[rows, cols] = term if v == 0 else num[rows, cols] + term
 
-    for v in range(2):
-        receive_taps(v)
-        row_pass(v, jnp.int32(0))
-
-        def cell_row(step, carry):
-            row_pass(v, step)
-            col_pass(v, step - 1)
-            if v == 1:
-                for n, ready in enumerate((2, 3, 5)):
-
-                    @pl.when(step == ready)
-                    def _():
-                        num_copies[n].start()
-
-            return carry
-
-        lax.fori_loop(1, CPS, cell_row, 0)
-        col_pass(v, jnp.int32(CPS - 1))
+    def cell_row(v, step):
+        row_pass(v, step)
+        col_pass(v, step - 1)
+
+    receive_taps(0, 0, EARLY, s_copies[0])
+    row_pass(0, jnp.int32(0))
+
+    @pl.loop(1, EARLY // CPS)
+    def _(step):
+        cell_row(0, step)
+
+    receive_taps(0, EARLY, PAD - EARLY, s_copies[1])
+
+    @pl.loop(EARLY // CPS, CPS)
+    def _(step):
+        cell_row(0, step)
+
+    col_pass(0, jnp.int32(CPS - 1))
+
+    receive_taps(1, 0, PAD, s_copies[2])
+    row_pass(1, jnp.int32(0))
+    num_copies = [
+        share_part(0, 0, 64, 0), share_part(0, 64, 32, 1), share_part(1, 0, 96, 2),
+        share_part(2, 0, 64, 3), share_part(2, 64, 32, 4),
+    ]
+
+    @pl.loop(1, CPS)
+    def _(step):
+        cell_row(1, step)
+        for n, copy in enumerate(num_copies):
+
+            @pl.when(step == n + 1)
+            def _():
+                copy.start()
+
+    col_pass(1, jnp.int32(CPS - 1))
 
     mine = pl.ds(pl.multiple_of(x * SHARE, SHARE), SHARE)
     for copy in den_copies + num_copies:
@@ -408,7 +445,7 @@
 
     for copy in z_first + z_up + z_down + cs_copies + [h_down, h_up] + x_copies:
         copy.wait_send()
-    for copy in s_copies[0] + s_copies[1] + den_copies + num_copies:
+    for copy in s_copies[0] + s_copies[1] + s_copies[2] + den_copies + num_copies:
         copy.wait_send()
 
 
@@ -446,9 +483,9 @@
             dma((5,)),
             dma((2, N_LINE)), dma((2, N_LINE)),
             dma((N_LINE,)), dma((N_LINE,)),
-            dma((2, N_LINE)), dma((2, N_LINE)),
+            dma((3, N_LINE)), dma((3, N_LINE)),
             dma((2,)), dma((2,)), dma((2,)), dma((2,)),
-            dma((3,)), dma((3,)), dma((3,)), dma((3,)),
+            dma((5,)), dma((5,)), dma((3,)), dma((3,)),
         ],
         compiler_params=pltpu.CompilerParams(
             collective_id=0, has_side_effects=True, vmem_limit_bytes=60 * 1024 * 1024

time: 54.2 us -> 50.5 us (0.932)
  Pallas kernels: 51.7 us -> 48 us
    pallas_call x1, Pallas kernels: 51.7 us -> 48 us  [shards(): pl.pallas_call(kernel, out_shape=(out, out), in_specs=[pl.BlockSpec(memor...]
where the time goes in v3:
time: 50.5 us; the launch traced here: 50.3 us
  Pallas kernels  48 us (95%)
  other arithmetic  1.71 us (3%)
  between operations  0.64 us (1%)
    pallas_call x1, Pallas kernels, shards(): pl.pallas_call(kernel, out_shape=(out, out), in_specs=[pl.BlockSpec(memor...  48 us
    div x1, other arithmetic, shards(): return (top_sum / weight_sum, weight_sum)  1.71 us

profile of v3, /device:TPU:1, one launch (start us, length us, event | category | flops | bytes accessed | tf_op | source)
XLA Modules:
  0.0 50.3 jit_solution(11157913935943882348)
XLA Ops:
  0.6 48.0 %shard_map.68 = (f32[96,384]{1,0:T(8,128)}, f32[96,384]{1,0:T(8,128)}) custom-call(f32[2,384,384]{2,1,0:T(8,128)} %img.1, f32[2,384,384]{2,1,0:T(8,128)} %var_in.1, f32[36,2,246]{2,1,0:T(2,128)} %bitcast.1, s32[2,36]{1,0:T(2,128)} %cs_in.1, s32[2,36]{1,0:T(2,128)} %cov_in.1), custom_call_target="tpu_custom_call" | custom-call | tf_op jit(solution)/shard_map/pallas_call | solution.py:456
  48.6 1.7 %fusion = (f32[96,384]{1,0:T(8,128)}, f32[96,384]{1,0:T(8,128)}) fusion(f32[96,384]{1,0:T(8,128)} %get-tuple-element.4, f32[96,384]{1,0:T(8,128)} %get-tuple-element.5), kind=kLoop, calls=%fused_computation.1 | loop fusion | flops 73728 | bytes 589824 | tf_op jit(solution)/shard_map/div | solution.py:495

commit v4 on v3

--- a/solution.py
+++ b/solution.py
@@ -18,10 +18,12 @@
 ROWS = SIDE + 2 * BORDER
 WINDOW = 80
 SHARE = 96
-EARLY = 16
+SLICE = 32
+LINE = 384
 CHUNK = 72
 N_VERT = 4
 N_LINE = 8
+STORE = N_LINE * LINE
 
 MESH = pl.DeviceIdType.MESH
 f32 = jnp.float32
@@ -46,9 +48,9 @@
 def kernel(
     img, var_in, fac_in, cs_in, cov_in,
     top_sum, weight_sum,
-    ext, var, fac, cs, cov, zbuf, csb, hot, sbuf, rbuf, taps, xs, xr, thi, tlo, weight, num, den,
+    ext, var, fac, cs, cov, cells, slices, column, packed, hot, sbuf, rbuf, taps, xs, xr, thi, tlo, weight, num, den,
     rnum, rden, halves,
-    in_sem, zsend, zrecv, csend, crecv, ssend, srecv, hsend, hrecv, xsend, xrecv,
+    in_sem, zsend, zrecv, psend, precv, ssend, srecv, hsend, hrecv, xsend, xrecv,
     nsend, nrecv, dsend, drecv,
 ):
     a = lax.axis_index("py")
@@ -87,27 +89,25 @@
         copy.start()
 
     inputs[0].wait()
+    cells[...] = jnp.zeros((128, 256), f32)
     for v in range(2):
-        zbuf[v, 0] = jnp.zeros((PAD, 256), f32)
-        zbuf[v, 0, 0:CELLS, 0:FACT] = fac[:, v, :]
+        cells[CELLS * v:CELLS * (v + 1), 0:FACT] = fac[:, v, :]
+    for n in range(2):
+        slices[4 * n:4 * (n + 1), 0:SLICE] = cells[:, 128 * n:128 * (n + 1)].T.reshape(4, SLICE, 128)
     inputs[1].wait()
-    csb[0] = jnp.full((8, 128), -1.0, f32)
-    csb[0, 0:2, 0:CELLS] = cs[...].astype(f32)
+    slices[:, SLICE:SLICE + 8] = jnp.full((N_LINE, 8, 128), -1.0, f32)
+    for n in range(N_LINE):
+        slices[n, SLICE:SLICE + 2, 0:CELLS] = cs[...].astype(f32)
+    column[a] = slices[a]
 
     pl.semaphore_wait(barrier, 2 * (N_LINE - 1) + N_VERT - 1)
 
-    def ring(v, source, target, d):
-        return remote(
-            zbuf.at[v, source], zbuf.at[v, target], zsend.at[v, target], zrecv.at[v, target],
+    z_copies = [
+        remote(
+            slices.at[lax.rem(a + d, N_LINE)], column.at[a], zsend.at[d], zrecv.at[N_LINE - d],
             at_py(d),
         )
-
-    z_first = [ring(0, 0, d, d) for d in (4, 3, 5, 2, 6, 1, 7)]
-    z_up = [ring(1, s, t, 1) for s, t in ((0, 1), (1, 2), (2, 3), (3, 4))]
-    z_down = [ring(1, s, t, N_LINE - 1) for s, t in ((0, 7), (7, 6), (6, 5))]
-    cs_copies = [
-        remote(csb.at[0], csb.at[N_LINE - d], csend.at[d], crecv.at[N_LINE - d], at_px(d))
-        for d in range(1, N_LINE)
+        for d in (4, 3, 5, 2, 6, 1, 7)
     ]
     h_down = remote(
         img.at[:, pl.ds(SIDE - BORDER, BORDER), :], ext.at[:, pl.ds(0, BORDER), :],
@@ -117,15 +117,8 @@
         img.at[:, pl.ds(0, BORDER), :], ext.at[:, pl.ds(BORDER + SIDE, BORDER), :],
         hsend.at[1], hrecv.at[1], at_py(N_LINE - 1),
     )
-    for copy in [h_down, h_up] + z_first + cs_copies + [z_up[0], z_down[0]]:
+    for copy in z_copies + [h_down, h_up]:
         copy.start()
-
-    def pass_on(step):
-        z_up[step - 1].wait_recv()
-        z_up[step].start()
-        if step < 3:
-            z_down[step - 1].wait_recv()
-            z_down[step].start()
 
     inputs[2].wait()
     inputs[3].wait()
@@ -143,6 +136,7 @@
                 weight[v, rows, cols] = w
                 total = total + w
             den[rows, cols] = total
+            num[rows, cols] = jnp.zeros((CELL, 128), f32)
         return carry
 
     lax.fori_loop(0, CPS, weight_rows, 0)
@@ -166,6 +160,32 @@
             num.at[pl.ds(base, count)], rnum.at[n, pl.ds(first, count)],
             nsend.at[sem], nrecv.at[sem], {"vert": t},
         )
+
+    for copy in z_copies:
+        copy.wait_recv()
+    lane = lanes(SLICE)
+
+    def gather_tiles(v):
+        for t in range(3):
+            tile = jnp.zeros((SLICE, 128), f32)
+            for i in range(min(3, N_LINE - 3 * t)):
+                inside = (lane >= CELLS * i) & (lane < CELLS * (i + 1))
+                part = turn(column[3 * t + i, 0:SLICE], CELLS * (i - v))
+                tile = jnp.where(inside, part, tile)
+            packed[b, v, :, 128 * t:128 * (t + 1)] = tile
+
+    p_copies = [
+        [
+            remote(
+                packed.at[b, v], packed.at[b, v], psend.at[v, d], precv.at[v, N_LINE - d], at_px(d)
+            )
+            for d in range(1, N_LINE)
+        ]
+        for v in range(2)
+    ]
+    gather_tiles(0)
+    for copy in p_copies[0]:
+        copy.start()
 
     inputs[4].wait()
     h_down.wait_recv()
@@ -200,55 +220,66 @@
     for copy in x_copies:
         copy.start()
 
-    pass_on(1)
-
-    for copy in cs_copies:
-        copy.wait_recv()
-    names = csb[...].reshape(8 * N_LINE, 128)
+    gather_tiles(1)
+    for copy in p_copies[1]:
+        copy.start()
+
+    names = jnp.concatenate(
+        [column[lax.rem(a + d, N_LINE), SLICE:SLICE + 8] for d in range(N_LINE)], axis=0
+    )
     wanted = jnp.concatenate([names, names], axis=0).T
-    lane = lax.broadcasted_iota(jnp.int32, (1, 384), 1)
-    behind = jnp.zeros((1, 384), jnp.int32)
-    for n in range(1, N_LINE):
-        behind = behind + (lane >= PAD * n).astype(jnp.int32)
-    slot = lane - PAD * behind
-    owner = (a - behind + N_LINE) & (N_LINE - 1)
-    stored = ((owner * N_LINE + b) * CELLS + slot).astype(f32)
-    stored = jnp.where(slot < CELLS, stored, -2.0)
+    lane = lax.broadcasted_iota(jnp.int32, (1, LINE), 1)
+    tile = (lane >= 128).astype(jnp.int32) + (lane >= 256).astype(jnp.int32)
+    lane = lane - 128 * tile
+    place = (lane >= CELLS).astype(jnp.int32) + (lane >= 2 * CELLS).astype(jnp.int32)
+    owner = 3 * tile + place
+    stored = owner * (N_LINE * CELLS) + (lane - CELLS * place)
+    held = (lane < 3 * CELLS) & (owner < N_LINE)
+    stored = jnp.concatenate(
+        [jnp.where(held, stored + CELLS * n, -2) for n in range(N_LINE)], axis=1
+    ).astype(f32)
     for v in range(2):
-        hot[v] = jnp.concatenate(
-            [
-                jnp.where(wanted[0:PAD, 8 * d + v:8 * d + v + 1] == stored, 1.0, 0.0)
-                for d in range(N_LINE)
-            ],
-            axis=0,
-        ).astype(bf16)
-    pass_on(2)
-
-    def pick_copies(v, first, count, sem):
-        rows = pl.ds(first, count)
-        return [
+        for d in range(0, N_LINE, 2):
+            hot[v, PAD * d:PAD * (d + 2)] = jnp.concatenate(
+                [
+                    jnp.where(wanted[0:PAD, 8 * n + v:8 * n + v + 1] == stored, 1.0, 0.0)
+                    for n in (d, d + 1)
+                ],
+                axis=0,
+            ).astype(bf16)
+
+    s_copies = [
+        [
             remote(
-                sbuf.at[v, d, rows], rbuf.at[v, N_LINE - d, rows], ssend.at[sem, d],
-                srecv.at[sem, N_LINE - d], at_px(d),
-            )
-            for d in range(1, N_LINE)
+                sbuf.at[v, d], rbuf.at[v, a], ssend.at[v, d], srecv.at[v, N_LINE - d], at_py(d)
+            )
+            for d in (4, 3, 5, 2, 6, 1, 7)
         ]
-
-    s_copies = [pick_copies(0, 0, EARLY, 0), pick_copies(0, EARLY, PAD - EARLY, 1), pick_copies(1, 0, PAD, 2)]
+        for v in range(2)
+    ]
 
     def pick(v):
-        high, low = split(zbuf[v].reshape(N_LINE * PAD, 256))
-        table = jnp.concatenate([high, low], axis=1)
-        table = jnp.concatenate([table, jnp.zeros((384 - N_LINE * PAD, 512), bf16)], axis=0)
-        picked = jnp.dot(hot[v], table, preferred_element_type=f32)
-        sbuf[v] = (picked[:, 0:256] + picked[:, 256:512]).reshape(N_LINE, PAD, 256)
-
-    for copy in z_first:
-        copy.wait_recv()
+        for copy in p_copies[v]:
+            copy.wait_recv()
+        high, low = split(jnp.concatenate([packed[n, v] for n in range(N_LINE)], axis=1))
+        table = jnp.concatenate([high, low, jnp.zeros((64, STORE), bf16)], axis=0)
+        picked = lax.dot_general(
+            hot[v], table, (((1,), (1,)), ((), ())), preferred_element_type=f32
+        )
+        picked = picked + turn(picked, -SLICE)
+        groups = picked.reshape(N_LINE, 5, 8, 128)
+        groups = [groups[:, g].reshape(8 * N_LINE, 128) for g in range(5)]
+        lane = lanes(8 * N_LINE)
+        first = groups[0]
+        for g in range(1, 4):
+            first = jnp.where(lane < SLICE * g, first, turn(groups[g], SLICE * g))
+        sbuf[v, :, 0:8] = first.reshape(N_LINE, 8, 128)
+        sbuf[v, :, 8:16] = groups[4].reshape(N_LINE, 8, 128)
+        rbuf[v, a] = sbuf[v, 0]
+        for copy in s_copies[v]:
+            copy.start()
+
     pick(0)
-    for copy in s_copies[0] + s_copies[1]:
-        copy.start()
-    pass_on(3)
 
     for copy in x_copies:
         copy.wait_recv()
@@ -283,33 +314,36 @@
 
     tiles(0)
     tiles(1)
-
-    for copy in (z_up[3], z_down[2]):
-        copy.wait_recv()
     pick(1)
-    for copy in s_copies[2]:
-        copy.start()
 
     half = CELL // 2
 
-    def receive_taps(v, first, count, copies):
-        for copy in copies:
+    def receive_taps(v):
+        for copy in s_copies[v]:
             copy.wait_recv()
-        rows = slice(first, first + count)
-        total = sbuf[v, 0, rows]
-        for d in range(1, N_LINE):
-            total = total + rbuf[v, d, rows]
-        lane = lanes(count)
+        lane = lanes(8)
+        total = []
+        for n in range(2):
+            groups = []
+            for g in range(5):
+                rows, shift = (slice(0, 8), SLICE * g) if g < 4 else (slice(8, 16), 0)
+                piece = turn(rbuf[v, 4 * n, rows], -shift)
+                for i in range(1, 4):
+                    other = turn(rbuf[v, 4 * n + i, rows], SLICE * i - shift)
+                    piece = jnp.where(lane < SLICE * i, piece, other)
+                groups.append(piece)
+            total.append(jnp.concatenate(groups, axis=0))
+        lane = lanes(PAD)
         for p in range(2 * RANK):
             n, offset = divmod(TAPS * p, 128)
-            tap = turn(total[:, 128 * n:128 * (n + 1)], -offset)
+            tap = turn(total[n], -offset)
             if offset + TAPS > 128:
-                rest = turn(total[:, 128 * (n + 1):128 * (n + 2)], -offset)
+                rest = turn(total[n + 1], -offset)
                 tap = jnp.where(lane < 128 - offset, tap, rest)
             tap = jnp.where(lane < TAPS, tap, 0.0)
             high = tap.astype(bf16).astype(f32)
-            taps[v, p, 0, rows] = high
-            taps[v, p, 1, rows] = tap - high
+            taps[v, p, 0] = high
+            taps[v, p, 1] = tap - high
 
     def band(v, p, part, q, count, shift):
         row = jnp.broadcast_to(taps[v, p, part, pl.ds(q, 1), :], (count, 128))
@@ -344,18 +378,17 @@
             axis=0,
         ).astype(bf16)
 
-    def row_of(v, step):
-        if v == 0:
-            return step
-        late = step // 3
-        place = step - 3 * late
+    def visit_and_row(step):
+        late = step // 6
+        visit = lax.rem(step // 3, 2)
+        place = lax.rem(step, 3)
         flip = lax.rem(x + late, 2)
         place = place + flip * (2 - 2 * place)
         side = x // 2
-        return 3 * ((1 - side) * (1 - late) + side * late) + place
-
-    def row_pass(v, step):
-        r = row_of(v, step)
+        return visit, 3 * ((1 - side) * (1 - late) + side * late) + place
+
+    def row_pass(step):
+        v, r = visit_and_row(step)
         top = pl.multiple_of(r * CELL, CELL)
         for c in range(CPS):
             windows = []
@@ -384,8 +417,8 @@
                 axis=0,
             )
 
-    def col_pass(v, step):
-        r = row_of(v, step)
+    def col_pass(step):
+        v, r = visit_and_row(step)
         rows = pl.ds(pl.multiple_of(r * CELL, CELL), CELL)
         for c in range(0, CPS, 2):
             pair = []
@@ -398,44 +431,34 @@
                 pair.append(both + turn(both, CELL))
             cols = slice(CELL * c, CELL * c + 128)
             term = weight[v, rows, cols] * jnp.where(lanes(CELL) < CELL, pair[0], pair[1])
-            num[rows, cols] = term if v == 0 else num[rows, cols] + term
-
-    def cell_row(v, step):
-        row_pass(v, step)
-        col_pass(v, step - 1)
-
-    receive_taps(0, 0, EARLY, s_copies[0])
-    row_pass(0, jnp.int32(0))
-
-    @pl.loop(1, EARLY // CPS)
-    def _(step):
-        cell_row(0, step)
-
-    receive_taps(0, EARLY, PAD - EARLY, s_copies[1])
-
-    @pl.loop(EARLY // CPS, CPS)
-    def _(step):
-        cell_row(0, step)
-
-    col_pass(0, jnp.int32(CPS - 1))
-
-    receive_taps(1, 0, PAD, s_copies[2])
-    row_pass(1, jnp.int32(0))
+            num[rows, cols] = num[rows, cols] + term
+
     num_copies = [
         share_part(0, 0, 64, 0), share_part(0, 64, 32, 1), share_part(1, 0, 96, 2),
         share_part(2, 0, 64, 3), share_part(2, 64, 32, 4),
     ]
 
-    @pl.loop(1, CPS)
+    receive_taps(0)
+    row_pass(jnp.int32(0))
+
+    @pl.loop(1, 3)
     def _(step):
-        cell_row(1, step)
-        for n, copy in enumerate(num_copies):
-
-            @pl.when(step == n + 1)
+        row_pass(step)
+        col_pass(step - 1)
+
+    receive_taps(1)
+
+    @pl.loop(3, 2 * CPS)
+    def _(step):
+        row_pass(step)
+        col_pass(step - 1)
+        for copy, ready in zip(num_copies, (4, 5, 6, 10, 11)):
+
+            @pl.when(step == ready)
             def _():
                 copy.start()
 
-    col_pass(1, jnp.int32(CPS - 1))
+    col_pass(jnp.int32(2 * CPS - 1))
 
     mine = pl.ds(pl.multiple_of(x * SHARE, SHARE), SHARE)
     for copy in den_copies + num_copies:
@@ -443,9 +466,9 @@
     weight_sum[...] = (den[mine] + rden[1]) + (rden[0] + rden[2])
     top_sum[...] = (num[mine] + rnum[1]) + (rnum[0] + rnum[2])
 
-    for copy in z_first + z_up + z_down + cs_copies + [h_down, h_up] + x_copies:
+    for copy in z_copies + [h_down, h_up] + x_copies + p_copies[0] + p_copies[1]:
         copy.wait_send()
-    for copy in s_copies[0] + s_copies[1] + s_copies[2] + den_copies + num_copies:
+    for copy in s_copies[0] + s_copies[1] + den_copies + num_copies:
         copy.wait_send()
 
 
@@ -464,11 +487,13 @@
             pltpu.VMEM((CELLS, 2, FACT), f32),
             pltpu.VMEM((2, CELLS), jnp.int32),
             pltpu.SMEM((2, CELLS), jnp.int32),
-            pltpu.VMEM((2, N_LINE, PAD, 256), f32),
-            pltpu.VMEM((N_LINE, 8, 128), f32),
-            pltpu.VMEM((2, N_LINE * PAD, 384), bf16),
-            pltpu.VMEM((2, N_LINE, PAD, 256), f32),
-            pltpu.VMEM((2, N_LINE, PAD, 256), f32),
+            pltpu.VMEM((128, 256), f32),
+            pltpu.VMEM((N_LINE, SLICE + 8, 128), f32),
+            pltpu.VMEM((N_LINE, SLICE + 8, 128), f32),
+            pltpu.VMEM((N_LINE, 2, SLICE, LINE), f32),
+            pltpu.VMEM((2, N_LINE * PAD, STORE), bf16),
+            pltpu.VMEM((2, N_LINE, 16, 128), f32),
+            pltpu.VMEM((2, N_LINE, 16, 128), f32),
             pltpu.VMEM((2, 2 * RANK, 2, PAD, 128), f32),
             pltpu.VMEM((2, 2, CHUNK, 128), f32),
             pltpu.VMEM((2, 2, CHUNK, 128), f32),
@@ -481,9 +506,9 @@
             pltpu.VMEM((N_VERT - 1, SHARE, SIDE), f32),
             pltpu.VMEM((2 * CPS, 128, 384), bf16),
             dma((5,)),
+            dma((N_LINE,)), dma((N_LINE,)),
             dma((2, N_LINE)), dma((2, N_LINE)),
-            dma((N_LINE,)), dma((N_LINE,)),
-            dma((3, N_LINE)), dma((3, N_LINE)),
+            dma((2, N_LINE)), dma((2, N_LINE)),
             dma((2,)), dma((2,)), dma((2,)), dma((2,)),
             dma((5,)), dma((5,)), dma((3,)), dma((3,)),
         ],

time: 50.5 us -> 47.6 us (0.943)
  Pallas kernels: 48 us -> 45.1 us
    pallas_call x1, Pallas kernels: 48 us -> 45.1 us  [shards(): pl.pallas_call(kernel, out_shape=(out, out), in_specs=[pl.BlockSpec(memor...]
where the time goes in v4:
time: 47.6 us; the launch traced here: 47.5 us
  Pallas kernels  45.1 us (95%)
  other arithmetic  1.71 us (4%)
  between operations  0.64 us (1%)
    pallas_call x1, Pallas kernels, shards(): pl.pallas_call(kernel, out_shape=(out, out), in_specs=[pl.BlockSpec(memor...  45.1 us
    div x1, other arithmetic, shards(): return (top_sum / weight_sum, weight_sum)  1.71 us

profile of v4, /device:TPU:1, one launch (start us, length us, event | category | flops | bytes accessed | tf_op | source)
XLA Modules:
  0.0 47.5 jit_solution(5647741849262184420)
XLA Ops:
  0.6 45.1 %shard_map.68 = (f32[96,384]{1,0:T(8,128)}, f32[96,384]{1,0:T(8,128)}) custom-call(f32[2,384,384]{2,1,0:T(8,128)} %img.1, f32[2,384,384]{2,1,0:T(8,128)} %var_in.1, f32[36,2,246]{2,1,0:T(2,128)} %bitcast.1, s32[2,36]{1,0:T(2,128)} %cs_in.1, s32[2,36]{1,0:T(2,128)} %cov_in.1), custom_call_target="tpu_custom_call" | custom-call | tf_op jit(solution)/shard_map/pallas_call | solution.py:479
  45.7 1.7 %fusion = (f32[96,384]{1,0:T(8,128)}, f32[96,384]{1,0:T(8,128)}) fusion(f32[96,384]{1,0:T(8,128)} %get-tuple-element.4, f32[96,384]{1,0:T(8,128)} %get-tuple-element.5), kind=kLoop, calls=%fused_computation.1 | loop fusion | flops 73728 | bytes 589824 | tf_op jit(solution)/shard_map/div | solution.py:520

commit v5 on v4

--- a/solution.py
+++ b/solution.py
@@ -23,6 +23,7 @@
 CHUNK = 72
 N_VERT = 4
 N_LINE = 8
+FAR_FIRST = (4, 5, 3, 6, 2, 7, 1)
 STORE = N_LINE * LINE
 
 MESH = pl.DeviceIdType.MESH
@@ -71,7 +72,7 @@
         )
 
     barrier = pltpu.get_barrier_semaphore()
-    for d in range(1, N_LINE):
+    for d in FAR_FIRST:
         pl.semaphore_signal(barrier, inc=1, device_id=at_py(d), device_id_type=MESH)
     for d in range(1, N_LINE):
         pl.semaphore_signal(barrier, inc=1, device_id=at_px(d), device_id_type=MESH)
@@ -107,7 +108,7 @@
             slices.at[lax.rem(a + d, N_LINE)], column.at[a], zsend.at[d], zrecv.at[N_LINE - d],
             at_py(d),
         )
-        for d in (4, 3, 5, 2, 6, 1, 7)
+        for d in FAR_FIRST
     ]
     h_down = remote(
         img.at[:, pl.ds(SIDE - BORDER, BORDER), :], ext.at[:, pl.ds(0, BORDER), :],
@@ -179,45 +180,12 @@
             remote(
                 packed.at[b, v], packed.at[b, v], psend.at[v, d], precv.at[v, N_LINE - d], at_px(d)
             )
-            for d in range(1, N_LINE)
+            for d in FAR_FIRST
         ]
         for v in range(2)
     ]
     gather_tiles(0)
     for copy in p_copies[0]:
-        copy.start()
-
-    inputs[4].wait()
-    h_down.wait_recv()
-    h_up.wait_recv()
-
-    @pl.when(a == 0)
-    def _():
-        ext[:, 0:BORDER, :] = jnp.zeros((2, BORDER, SIDE), f32)
-
-    @pl.when(a == N_LINE - 1)
-    def _():
-        ext[:, BORDER + SIDE:ROWS, :] = jnp.zeros((2, BORDER, SIDE), f32)
-
-    def pack(v, carry):
-        lane = lanes(CHUNK)
-        last = jnp.zeros((CHUNK, 128), f32)
-        first = jnp.zeros((CHUNK, 128), f32)
-        for g in range(ROWS // CHUNK):
-            inside = (lane >= HALF * g) & (lane < HALF * (g + 1))
-            rows = slice(CHUNK * g, CHUNK * (g + 1))
-            last = jnp.where(inside, turn(ext[v, rows, 256:384], HALF * g - 108), last)
-            first = jnp.where(inside, turn(ext[v, rows, 0:128], HALF * g), first)
-        xs[0, v] = last
-        xs[1, v] = first
-        return carry
-
-    lax.fori_loop(0, 2, pack, 0)
-    x_copies = [
-        remote(xs.at[0], xr.at[0], xsend.at[0], xrecv.at[0], at_px(1)),
-        remote(xs.at[1], xr.at[1], xsend.at[1], xrecv.at[1], at_px(N_LINE - 1)),
-    ]
-    for copy in x_copies:
         copy.start()
 
     gather_tiles(1)
@@ -248,12 +216,45 @@
                 axis=0,
             ).astype(bf16)
 
+    inputs[4].wait()
+    h_down.wait_recv()
+    h_up.wait_recv()
+
+    @pl.when(a == 0)
+    def _():
+        ext[:, 0:BORDER, :] = jnp.zeros((2, BORDER, SIDE), f32)
+
+    @pl.when(a == N_LINE - 1)
+    def _():
+        ext[:, BORDER + SIDE:ROWS, :] = jnp.zeros((2, BORDER, SIDE), f32)
+
+    def pack(v, carry):
+        lane = lanes(CHUNK)
+        last = jnp.zeros((CHUNK, 128), f32)
+        first = jnp.zeros((CHUNK, 128), f32)
+        for g in range(ROWS // CHUNK):
+            inside = (lane >= HALF * g) & (lane < HALF * (g + 1))
+            rows = slice(CHUNK * g, CHUNK * (g + 1))
+            last = jnp.where(inside, turn(ext[v, rows, 256:384], HALF * g - 108), last)
+            first = jnp.where(inside, turn(ext[v, rows, 0:128], HALF * g), first)
+        xs[0, v] = last
+        xs[1, v] = first
+        return carry
+
+    lax.fori_loop(0, 2, pack, 0)
+    x_copies = [
+        remote(xs.at[0], xr.at[0], xsend.at[0], xrecv.at[0], at_px(1)),
+        remote(xs.at[1], xr.at[1], xsend.at[1], xrecv.at[1], at_px(N_LINE - 1)),
+    ]
+    for copy in x_copies:
+        copy.start()
+
     s_copies = [
         [
             remote(
                 sbuf.at[v, d], rbuf.at[v, a], ssend.at[v, d], srecv.at[v, N_LINE - d], at_py(d)
             )
-            for d in (4, 3, 5, 2, 6, 1, 7)
+            for d in FAR_FIRST
         ]
         for v in range(2)
     ]
@@ -280,6 +281,7 @@
             copy.start()
 
     pick(0)
+    pick(1)
 
     for copy in x_copies:
         copy.wait_recv()
@@ -314,7 +316,6 @@
 
     tiles(0)
     tiles(1)
-    pick(1)
 
     half = CELL // 2
 
@@ -380,8 +381,9 @@
 
     def visit_and_row(step):
         late = step // 6
-        visit = lax.rem(step // 3, 2)
-        place = lax.rem(step, 3)
+        here = step - 6 * late
+        visit = (1 - late) * (here // 3) + late * lax.rem(here, 2)
+        place = (1 - late) * lax.rem(here, 3) + late * (here // 2)
         flip = lax.rem(x + late, 2)
         place = place + flip * (2 - 2 * place)
         side = x // 2
@@ -452,7 +454,7 @@
     def _(step):
         row_pass(step)
         col_pass(step - 1)
-        for copy, ready in zip(num_copies, (4, 5, 6, 10, 11)):
+        for copy, ready in zip(num_copies, (4, 5, 6, 8, 10)):
 
             @pl.when(step == ready)
             def _():

time: 47.6 us -> 46.3 us (0.973)
  Pallas kernels: 45.1 us -> 43.8 us
    pallas_call x1, Pallas kernels: 45.1 us -> 43.8 us  [shards(): pl.pallas_call(kernel, out_shape=(out, out), in_specs=[pl.BlockSpec(memor...]
where the time goes in v5:
time: 46.3 us; the launch traced here: 46.1 us
  Pallas kernels  43.8 us (95%)
  other arithmetic  1.71 us (4%)
  between operations  0.64 us (1%)
    pallas_call x1, Pallas kernels, shards(): pl.pallas_call(kernel, out_shape=(out, out), in_specs=[pl.BlockSpec(memor...  43.8 us
    div x1, other arithmetic, shards(): return (top_sum / weight_sum, weight_sum)  1.71 us

profile of v5, /device:TPU:1, one launch (start us, length us, event | category | flops | bytes accessed | tf_op | source)
XLA Modules:
  0.0 46.1 jit_solution(1353585333321000334)
XLA Ops:
  0.6 43.8 %shard_map.68 = (f32[96,384]{1,0:T(8,128)}, f32[96,384]{1,0:T(8,128)}) custom-call(f32[2,384,384]{2,1,0:T(8,128)} %img.1, f32[2,384,384]{2,1,0:T(8,128)} %var_in.1, f32[36,2,246]{2,1,0:T(2,128)} %bitcast.1, s32[2,36]{1,0:T(2,128)} %cs_in.1, s32[2,36]{1,0:T(2,128)} %cov_in.1), custom_call_target="tpu_custom_call" | custom-call | tf_op jit(solution)/shard_map/pallas_call | solution.py:481
  44.4 1.7 %fusion = (f32[96,384]{1,0:T(8,128)}, f32[96,384]{1,0:T(8,128)}) fusion(f32[96,384]{1,0:T(8,128)} %get-tuple-element.4, f32[96,384]{1,0:T(8,128)} %get-tuple-element.5), kind=kLoop, calls=%fused_computation.1 | loop fusion | flops 73728 | bytes 589824 | tf_op jit(solution)/shard_map/div | solution.py:522

commit v6 on v5

--- a/solution.py
+++ b/solution.py
@@ -18,6 +18,7 @@
 ROWS = SIDE + 2 * BORDER
 WINDOW = 80
 SHARE = 96
+EACH = 4
 SLICE = 32
 LINE = 384
 CHUNK = 72
@@ -380,14 +381,15 @@
         ).astype(bf16)
 
     def visit_and_row(step):
-        late = step // 6
-        here = step - 6 * late
-        visit = (1 - late) * (here // 3) + late * lax.rem(here, 2)
-        place = (1 - late) * lax.rem(here, 3) + late * (here // 2)
-        flip = lax.rem(x + late, 2)
+        late = step // (2 * EACH)
+        visit = (1 - late) * (step // EACH) + late * lax.rem(step, 2)
+        place = (1 - late) * lax.rem(step, EACH) + late * (step // 2)
+        near = place // 3
+        place = place - 3 * near
+        flip = lax.rem(x + near, 2)
         place = place + flip * (2 - 2 * place)
         side = x // 2
-        return visit, 3 * ((1 - side) * (1 - late) + side * late) + place
+        return visit, 3 * ((1 - side) * (1 - near) + side * near) + place
 
     def row_pass(step):
         v, r = visit_and_row(step)
@@ -443,18 +445,18 @@
     receive_taps(0)
     row_pass(jnp.int32(0))
 
-    @pl.loop(1, 3)
+    @pl.loop(1, EACH)
     def _(step):
         row_pass(step)
         col_pass(step - 1)
 
     receive_taps(1)
 
-    @pl.loop(3, 2 * CPS)
+    @pl.loop(EACH, 2 * CPS)
     def _(step):
         row_pass(step)
         col_pass(step - 1)
-        for copy, ready in zip(num_copies, (4, 5, 6, 8, 10)):
+        for copy, ready in zip(num_copies, (5, 6, 7, 8, 10)):
 
             @pl.when(step == ready)
             def _():

time: 46.3 us -> 45.6 us (0.985)
  Pallas kernels: 43.8 us -> 43.1 us
    pallas_call x1, Pallas kernels: 43.8 us -> 43.1 us  [shards(): pl.pallas_call(kernel, out_shape=(out, out), in_specs=[pl.BlockSpec(memor...]
where the time goes in v6:
time: 45.6 us; the launch traced here: 45.5 us
  Pallas kernels  43.1 us (95%)
  other arithmetic  1.71 us (4%)
  between operations  0.64 us (1%)
    pallas_call x1, Pallas kernels, shards(): pl.pallas_call(kernel, out_shape=(out, out), in_specs=[pl.BlockSpec(memor...  43.1 us
    div x1, other arithmetic, shards(): return (top_sum / weight_sum, weight_sum)  1.71 us

profile of v6, /device:TPU:1, one launch (start us, length us, event | category | flops | bytes accessed | tf_op | source)
XLA Modules:
  0.0 45.5 jit_solution(9499867528739087867)
XLA Ops:
  0.6 43.1 %shard_map.68 = (f32[96,384]{1,0:T(8,128)}, f32[96,384]{1,0:T(8,128)}) custom-call(f32[2,384,384]{2,1,0:T(8,128)} %img.1, f32[2,384,384]{2,1,0:T(8,128)} %var_in.1, f32[36,2,246]{2,1,0:T(2,128)} %bitcast.1, s32[2,36]{1,0:T(2,128)} %cs_in.1, s32[2,36]{1,0:T(2,128)} %cov_in.1), custom_call_target="tpu_custom_call" | custom-call | tf_op jit(solution)/shard_map/pallas_call | solution.py:483
  43.8 1.7 %fusion = (f32[96,384]{1,0:T(8,128)}, f32[96,384]{1,0:T(8,128)}) fusion(f32[96,384]{1,0:T(8,128)} %get-tuple-element.4, f32[96,384]{1,0:T(8,128)} %get-tuple-element.5), kind=kLoop, calls=%fused_computation.1 | loop fusion | flops 73728 | bytes 589824 | tf_op jit(solution)/shard_map/div | solution.py:524

commit v7 on v6

--- a/solution.py
+++ b/solution.py
@@ -336,6 +336,7 @@
                 groups.append(piece)
             total.append(jnp.concatenate(groups, axis=0))
         lane = lanes(PAD)
+        pieces = ([], [])
         for p in range(2 * RANK):
             n, offset = divmod(TAPS * p, 128)
             tap = turn(total[n], -offset)
@@ -344,8 +345,17 @@
                 tap = jnp.where(lane < 128 - offset, tap, rest)
             tap = jnp.where(lane < TAPS, tap, 0.0)
             high = tap.astype(bf16).astype(f32)
-            taps[v, p, 0] = high
-            taps[v, p, 1] = tap - high
+            pieces[p % 2].extend((high, tap - high))
+        spot = lax.broadcasted_iota(jnp.int32, (128, 128), 0) + lanes(128)
+        mirror = jnp.where((spot == 0) | (spot == 128), 1.0, 0.0).astype(bf16)
+        turned = jnp.dot(
+            jnp.concatenate(pieces[1], axis=0).astype(bf16), mirror, preferred_element_type=f32
+        )
+        for k in range(RANK):
+            for part in range(2):
+                n = 2 * k + part
+                taps[v, 2 * k, part] = pieces[0][n]
+                taps[v, 2 * k + 1, part] = turned[PAD * n:PAD * (n + 1)]
 
     def band(v, p, part, q, count, shift):
         row = jnp.broadcast_to(taps[v, p, part, pl.ds(q, 1), :], (count, 128))
@@ -370,15 +380,15 @@
         return jnp.concatenate(parts, axis=0).astype(bf16)
 
     def col_bands(v, q):
-        return jnp.concatenate(
-            [
-                jnp.concatenate(
-                    [band(v, 2 * k + 1, part, q, CELL, 0) for k in range(RANK)], axis=1
-                )
-                for part in range(2)
-            ],
-            axis=0,
-        ).astype(bf16)
+        reach = CELL + 2 * HALF
+        parts = []
+        for k in range(RANK):
+            high = band(v, 2 * k + 1, 0, q, reach, 0)
+            low = band(v, 2 * k + 1, 1, q, reach, CELL)
+            parts += [
+                jnp.where(lanes(reach) < CELL, high, low), jnp.zeros((128 - reach, 128), f32)
+            ]
+        return jnp.concatenate(parts, axis=0).astype(bf16)
 
     def visit_and_row(step):
         late = step // (2 * EACH)
@@ -427,9 +437,9 @@
         for c in range(0, CPS, 2):
             pair = []
             for n in (c, c + 1):
-                both = lax.dot_general(
+                both = jnp.dot(
                     halves[lax.rem(step, 2) * CPS + n], col_bands(v, r * CPS + n),
-                    (((1,), (1,)), ((), ())), preferred_element_type=f32,
+                    preferred_element_type=f32,
                 )
                 both = both[0:CELL] + both[CELL:2 * CELL]
                 pair.append(both + turn(both, CELL))

time: 45.6 us -> 45.3 us (level)
  Pallas kernels: 43.1 us -> 42.5 us
    pallas_call x1, Pallas kernels: 43.1 us -> 42.5 us  [shards(): pl.pallas_call(kernel, out_shape=(out, out), in_specs=[pl.BlockSpec(memor...]
where the time goes in v7:
time: 45.3 us; the launch traced here: 44.9 us
  Pallas kernels  42.5 us (94%)
  other arithmetic  1.71 us (4%)
  between operations  0.64 us (1%)
    pallas_call x1, Pallas kernels, shards(): pl.pallas_call(kernel, out_shape=(out, out), in_specs=[pl.BlockSpec(memor...  42.5 us
    div x1, other arithmetic, shards(): return (top_sum / weight_sum, weight_sum)  1.71 us

profile of v7, /device:TPU:1, one launch (start us, length us, event | category | flops | bytes accessed | tf_op | source)
XLA Modules:
  0.0 44.9 jit_solution(713676188181505017)
XLA Ops:
  0.6 42.5 %shard_map.68 = (f32[96,384]{1,0:T(8,128)}, f32[96,384]{1,0:T(8,128)}) custom-call(f32[2,384,384]{2,1,0:T(8,128)} %img.1, f32[2,384,384]{2,1,0:T(8,128)} %var_in.1, f32[36,2,246]{2,1,0:T(2,128)} %bitcast.1, s32[2,36]{1,0:T(2,128)} %cs_in.1, s32[2,36]{1,0:T(2,128)} %cov_in.1), custom_call_target="tpu_custom_call" | custom-call | tf_op jit(solution)/shard_map/pallas_call | solution.py:493
  43.2 1.7 %fusion = (f32[96,384]{1,0:T(8,128)}, f32[96,384]{1,0:T(8,128)}) fusion(f32[96,384]{1,0:T(8,128)} %get-tuple-element.4, f32[96,384]{1,0:T(8,128)} %get-tuple-element.5), kind=kLoop, calls=%fused_computation.1 | loop fusion | flops 73728 | bytes 589824 | tf_op jit(solution)/shard_map/div | solution.py:534

commit v8 on v7

--- a/solution.py
+++ b/solution.py
@@ -448,8 +448,8 @@
             num[rows, cols] = num[rows, cols] + term
 
     num_copies = [
-        share_part(0, 0, 64, 0), share_part(0, 64, 32, 1), share_part(1, 0, 96, 2),
-        share_part(2, 0, 64, 3), share_part(2, 64, 32, 4),
+        share_part(0, 0, 64, 0), share_part(0, 64, 32, 1), share_part(1, 64, 32, 2),
+        share_part(1, 0, 64, 3), share_part(2, 0, 64, 4), share_part(2, 64, 32, 5),
     ]
 
     receive_taps(0)
@@ -466,7 +466,7 @@
     def _(step):
         row_pass(step)
         col_pass(step - 1)
-        for copy, ready in zip(num_copies, (5, 6, 7, 8, 10)):
+        for copy, ready in zip(num_copies, (5, 6, 6, 7, 8, 10)):
 
             @pl.when(step == ready)
             def _():
@@ -524,7 +524,7 @@
             dma((2, N_LINE)), dma((2, N_LINE)),
             dma((2, N_LINE)), dma((2, N_LINE)),
             dma((2,)), dma((2,)), dma((2,)), dma((2,)),
-            dma((5,)), dma((5,)), dma((3,)), dma((3,)),
+            dma((6,)), dma((6,)), dma((3,)), dma((3,)),
         ],
         compiler_params=pltpu.CompilerParams(
             collective_id=0, has_side_effects=True, vmem_limit_bytes=60 * 1024 * 1024

time: 45.3 us -> 45.9 us (1.013)
  Pallas kernels: 42.5 us -> 43.4 us
    pallas_call x1, Pallas kernels: 42.5 us -> 43.4 us  [shards(): pl.pallas_call(kernel, out_shape=(out, out), in_specs=[pl.BlockSpec(memor...]
where the time goes in v8:
time: 45.9 us; the launch traced here: 45.8 us
  Pallas kernels  43.4 us (95%)
  other arithmetic  1.71 us (4%)
  between operations  0.64 us (1%)
    pallas_call x1, Pallas kernels, shards(): pl.pallas_call(kernel, out_shape=(out, out), in_specs=[pl.BlockSpec(memor...  43.4 us
    div x1, other arithmetic, shards(): return (top_sum / weight_sum, weight_sum)  1.71 us

profile of v8, /device:TPU:1, one launch (start us, length us, event | category | flops | bytes accessed | tf_op | source)
XLA Modules:
  0.0 45.8 jit_solution(18107798966222531585)
XLA Ops:
  0.6 43.4 %shard_map.68 = (f32[96,384]{1,0:T(8,128)}, f32[96,384]{1,0:T(8,128)}) custom-call(f32[2,384,384]{2,1,0:T(8,128)} %img.1, f32[2,384,384]{2,1,0:T(8,128)} %var_in.1, f32[36,2,246]{2,1,0:T(2,128)} %bitcast.1, s32[2,36]{1,0:T(2,128)} %cs_in.1, s32[2,36]{1,0:T(2,128)} %cov_in.1), custom_call_target="tpu_custom_call" | custom-call | tf_op jit(solution)/shard_map/pallas_call | solution.py:493
  44.1 1.7 %fusion = (f32[96,384]{1,0:T(8,128)}, f32[96,384]{1,0:T(8,128)}) fusion(f32[96,384]{1,0:T(8,128)} %get-tuple-element.4, f32[96,384]{1,0:T(8,128)} %get-tuple-element.5), kind=kLoop, calls=%fused_computation.1 | loop fusion | flops 73728 | bytes 589824 | tf_op jit(solution)/shard_map/div | solution.py:534

commit v9 on v6

--- a/solution.py
+++ b/solution.py
@@ -18,7 +18,7 @@
 ROWS = SIDE + 2 * BORDER
 WINDOW = 80
 SHARE = 96
-EACH = 4
+EACH = 5
 SLICE = 32
 LINE = 384
 CHUNK = 72
@@ -456,7 +456,7 @@
     def _(step):
         row_pass(step)
         col_pass(step - 1)
-        for copy, ready in zip(num_copies, (5, 6, 7, 8, 10)):
+        for copy, ready in zip(num_copies, (6, 7, 8, 9, 10)):
 
             @pl.when(step == ready)
             def _():

time: 45.6 us -> 45.6 us (level); the launches traced: 45.5 us -> 45 us
  Pallas kernels: 43.1 us -> 42.6 us
    pallas_call x1, Pallas kernels: 43.1 us -> 42.6 us  [shards(): pl.pallas_call(kernel, out_shape=(out, out), in_specs=[pl.BlockSpec(memor...]
where the time goes in v9:
time: 45.6 us; the launch traced here: 45 us
  Pallas kernels  42.6 us (93%)
  other arithmetic  1.71 us (4%)
  between operations  0.64 us (1%)
    pallas_call x1, Pallas kernels, shards(): pl.pallas_call(kernel, out_shape=(out, out), in_specs=[pl.BlockSpec(memor...  42.6 us
    div x1, other arithmetic, shards(): return (top_sum / weight_sum, weight_sum)  1.71 us

profile of v9, /device:TPU:1, one launch (start us, length us, event | category | flops | bytes accessed | tf_op | source)
XLA Modules:
  0.0 45.0 jit_solution(8840555754615451316)
XLA Ops:
  0.6 42.6 %shard_map.68 = (f32[96,384]{1,0:T(8,128)}, f32[96,384]{1,0:T(8,128)}) custom-call(f32[2,384,384]{2,1,0:T(8,128)} %img.1, f32[2,384,384]{2,1,0:T(8,128)} %var_in.1, f32[36,2,246]{2,1,0:T(2,128)} %bitcast.1, s32[2,36]{1,0:T(2,128)} %cs_in.1, s32[2,36]{1,0:T(2,128)} %cov_in.1), custom_call_target="tpu_custom_call" | custom-call | tf_op jit(solution)/shard_map/pallas_call | solution.py:483
  43.3 1.7 %fusion = (f32[96,384]{1,0:T(8,128)}, f32[96,384]{1,0:T(8,128)}) fusion(f32[96,384]{1,0:T(8,128)} %get-tuple-element.4, f32[96,384]{1,0:T(8,128)} %get-tuple-element.5), kind=kLoop, calls=%fused_computation.1 | loop fusion | flops 73728 | bytes 589824 | tf_op jit(solution)/shard_map/div | solution.py:524
